TPU v7x, 32 devices: a whole 2x2x4 slice. The times are simulated.
32 devices in a mesh: row: 2 (over core), col: 16 (over z, y, x).
Axes of the slice: x: 2, y: 2, z: 4, core: 2. Of those that a mesh axis runs over, the one named last changes fastest.
Arguments:
- panel_adj: float32 [14336, 512], P('row', 'col'), may hold values from -6 to 6
- inv_diag: float32 [512, 512], P('col'), may hold values from -0.25 to 0.25
- row_panel: float32 [512, 14336], P('row', 'col'), may hold values from -0.25 to 0.25
- trailing_adj: float32 [14336, 14336], P('row', 'col'), may hold values from -6 to 6
- trailing_factor: float32 [14336, 14336], P('row', 'col'), may hold values from -0.046875 to 0.046875
Outputs:
- trailing_new: float32 [14336, 14336], P('row', 'col')
- row_adj: float32 [512, 14336], P('row', 'col')
All inputs are finite; a program needn't handle non-finite values.
Results may differ from a plain program's by a relative error of at most 0.00007.
Values sent between devices are 32-bit elements; how exact they have to be, the bound alone decides.
No kernel may reach another device: no remote copies, remote signals or barrier semaphores. Data moves between devices by JAX's collectives and lax.ppermute only.
A program may use at most 192 MiB of HBM per device.

v0:
```python
import jax
import jax.numpy as jnp
from jax import lax
from jax.sharding import PartitionSpec as P


def local(panel_adj, inv_diag, row_panel, trailing_adj, trailing_factor):
    highest = lax.Precision.HIGHEST
    inverse_all = lax.all_gather(inv_diag, "col", axis=0, tiled=True)
    scaled = jnp.dot(
        lax.all_gather(panel_adj, "col", axis=1, tiled=True),
        inverse_all,
        precision=highest,
        preferred_element_type=jnp.float32,
    )
    trailing_new = trailing_adj - jnp.dot(
        scaled,
        lax.all_gather(row_panel, "row", axis=0, tiled=True),
        precision=highest,
        preferred_element_type=jnp.float32,
    )
    terms_local = lax.dot_general(
        scaled,
        trailing_factor,
        (((0,), (0,)), ((), ())),
        precision=highest,
        preferred_element_type=jnp.float32,
    )
    row_adj = lax.psum_scatter(terms_local, "row", scatter_dimension=0, tiled=True)
    return (trailing_new, row_adj)


def solution(mesh):
    placed = (P("row", "col"), P("col", None), P("row", "col"), P("row", "col"), P("row", "col"))
    return jax.shard_map(
        local,
        mesh=mesh,
        in_specs=placed,
        out_specs=(P("row", "col"), P("row", "col")),
        check_vma=False,
    )
```

profile of v0, /device:TPU:13, one launch (start us, length us, event | category | flops | bytes accessed | tf_op | source)
XLA Modules:
  0.0 429.0 jit_solution(3572738277747298919)
XLA Ops:
  7.2 0.0 all-gather.6.cloned.1.call-start
  7.2 0.7 all-gather.6.cloned.1.call-update
  7.9 0.0 all-gather.4.cloned.1.call-start
  7.9 0.7 all-gather.4.cloned.1.call-update
  8.6 0.0 all-gather.8.cloned.1.call-start
  8.7 0.7 all-gather.8.cloned.1.call-update
  9.4 0.0 reduce-scatter.2.cloned.1.call-start
  9.4 55.5 %all-gather.6.cloned.1.call-done = f32[512,512]{1,0:T(8,128)} async-done(((f32[32,512]{1,0:T(8,128)}), f32[512,512]{1,0:T(8,128)}) %all-gather.6.cloned.1.call-update) | async-done | bytes 1048592 | tf_op jit(solution)/shard_map/all_gather | solution.py:9
  65.0 173.4 %all-gather.4.cloned.1.call-done = f32[7168,512]{0,1:T(8,128)} async-done(((f32[7168,32]{0,1:T(8,128)}), f32[7168,512]{0,1:T(8,128)}) %all-gather.4.cloned.1.call-update) | async-done | bytes 14680080 | tf_op jit(solution)/shard_map/all_gather | solution.py:11
  238.4 27.6 %fusion = f32[7168,512]{1,0:T(8,128)S(1)} fusion(f32[7168,512]{0,1:T(8,128)} %all-gather.4.cloned.1.call-done, f32[512,512]{1,0:T(8,128)} %all-gather.6.cloned.1.call-done), kind=kOutput, calls=%fused_computation.1 | convolution fusion | flops 22548578304 | bytes 30408704 | tf_op jit(solution)/shard_map/dot_general | solution.py:10
  266.0 0.0 copy-start
  266.0 5.2 %copy-done = f32[7168,512]{1,0:T(8,128)} copy-done((f32[7168,512]{1,0:T(8,128)}, f32[7168,512]{1,0:T(8,128)S(1)}, u32[]{:S(2)}) %copy-start) | copy-done | bytes 14680088
  271.2 98.1 %fusion.1 = f32[512,896]{1,0:T(8,128)} fusion(f32[7168,512]{1,0:T(8,128)S(1)} %fusion, f32[7168,896]{1,0:T(8,128)} %param.9), kind=kOutput, calls=%fused_computation.2 | convolution fusion | flops 39460012032 | bytes 42205184 | tf_op jit(solution)/shard_map/dot_general | solution.py:22
  369.3 0.0 reduce-scatter.2.cloned.1.call-update
  369.3 0.0 all-gather.8.cloned.1.call-done
  369.4 53.1 %convolution_subtract_fusion = f32[7168,896]{1,0:T(8,128)} fusion(f32[7168,896]{1,0:T(8,128)} %param.8, f32[7168,512]{1,0:T(8,128)} %copy-done, f32[512,896]{1,0:T(8,128)} %all-gather.8.cloned.1.call-done), kind=kOutput, calls=%fused_computation | convolution fusion | flops 39466434560 | bytes 67895296 | tf_op jit(solution)/shard_map/dot_general | solution.py:16
  422.5 0.0 reduce-scatter.2.cloned.1.call-done
Async XLA Ops:
  7.2 57.8 %all-gather.6.cloned.1.call-start = ((), (), s32[]{:S(2)}) async-start(), calls=%async_computation.2 | async-start | bytes 1114112 | tf_op jit(solution)/shard_map/all_gather | solution.py:9
  7.9 230.5 %all-gather.4.cloned.1.call-start = ((), (), s32[]{:S(2)}) async-start(), calls=%async_computation.1 | async-start | bytes 15597568 | tf_op jit(solution)/shard_map/all_gather | solution.py:11
  8.6 360.7 %all-gather.8.cloned.1.call-start = ((), (), s32[]{:S(2)}) async-start(), calls=%async_computation.3 | async-start | bytes 2752512 | tf_op jit(solution)/shard_map/all_gather | solution.py:18
  9.4 413.1 %reduce-scatter.2.cloned.1.call-start = ((), (), s32[]{:S(2)}) async-start(), calls=%async_computation.4 | async-start | bytes 2752512 | tf_op jit(solution)/shard_map/reduce_scatter | solution.py:29
  266.0 5.2 %copy-start = (f32[7168,512]{1,0:T(8,128)}, f32[7168,512]{1,0:T(8,128)S(1)}, u32[]{:S(2)}) copy-start(f32[7168,512]{1,0:T(8,128)S(1)} %fusion) | copy-start | bytes 44040196
Sparse Core Ops, SparseCore 0:
  10.8 54.1 all-gather.5
  67.7 170.6 all-gather.3
  240.0 11.3 all-gather.7
  369.4 10.5 reduce-scatter.1
where the time goes:
time: 433 us; the launch traced here: 429 us
  waiting for transfers between devices  231 us (53%)
  matrix products  179 us (41%)
  between operations  13.8 us (3%)
  local copies, waits for them, and re-layouts  5.19 us (1%)
    all_gather x1, waiting for transfers between devices, local(): lax.all_gather(panel_adj, 'col', axis=1, tiled=True)  173 us
    dot_general x1, matrix products, local(): lax.dot_general(scaled, trailing_factor, (((0,), (0,)), ((), ())), precis...  98.1 us
    all_gather x1, waiting for transfers between devices, local(): inverse_all = lax.all_gather(inv_diag, 'col', axis=0, tiled=True)  55.5 us
    dot_general x1, matrix products, local(): jnp.dot(scaled, lax.all_gather(row_panel, 'row', axis=0, tiled=True), pre...  53.1 us
    dot_general x1, matrix products, local(): jnp.dot(lax.all_gather(panel_adj, 'col', axis=1, tiled=True), inverse_all...  27.6 us
  transfers between devices with their start and end apart: 4, of which 2 were waited for; matrix products, arithmetic and copies ran while one was open for 42% of the time, Pallas kernels for 0%

commit v1 on v0

v1 whole, which is shorter than its diff:
```python
import functools

import jax
import jax.numpy as jnp
from jax import lax
from jax.experimental import pallas as pl
from jax.experimental.pallas import tpu as pltpu
from jax.sharding import PartitionSpec as P

F32, BF16 = jnp.float32, jnp.bfloat16
VMEM_BYTES = 32 << 20
HIGHEST = lax.Precision.HIGHEST


def two_terms(x):
    high = x.astype(BF16)
    return high, (x - high.astype(F32)).astype(BF16)


def dot(a, b, dims=(((1,), (0,)), ((), ()))):
    return lax.dot_general(a, b, dims, preferred_element_type=F32)


def dot3(a, b, dims=(((1,), (0,)), ((), ()))):
    return dot(a[0], b[0], dims) + dot(a[0], b[1], dims) + dot(a[1], b[0], dims)


def panel_kernel(places, first, *refs):
    n = len(places)
    pieces, (factor, adj, w), refs = refs[:n], refs[n : n + 3], refs[n + 3 :]
    if not first:
        refs = refs[2:]
    out, sums, p_high, p_low, w_high, w_low = refs

    @pl.when(pl.program_id(0) == 0)
    def _():
        if first:
            sums[...] = jnp.zeros_like(sums)
        w_high[...], w_low[...] = two_terms(w[...])

    for piece, place in zip(pieces, places):
        high, low = two_terms(piece[...])
        for src, rows, dst in place:
            p_high[dst : dst + rows, :] = high[src : src + rows]
            p_low[dst : dst + rows, :] = low[src : src + rows]
    panel = p_high[...], p_low[...]
    sums[...] += dot3(panel, two_terms(factor[...]))
    out[...] = adj[...] - dot3(panel, (w_high[...], w_low[...]), (((0,), (0,)), ((), ())))


def panel_step(early, pieces, places, factor, adj, w, state, start, skip, size, tile):
    rows, cols = factor.shape
    depth = w.shape[0]
    at, off = start // tile, skip // tile
    held = pl.BlockSpec(memory_space=pltpu.VMEM)
    tiled = pl.BlockSpec((tile, cols), lambda i: (i + at, 0))
    n = len(early) + len(pieces)
    first = state is None
    args = [*early, *pieces, factor, adj, w]
    in_specs = [pl.BlockSpec((p.shape[0], tile), lambda i: (0, i + at)) for p in early]
    in_specs += [pl.BlockSpec((p.shape[0], tile), lambda i: (0, i + off)) for p in pieces] + [tiled, tiled, held]
    aliases = {}
    if not first:
        args += [state[1], state[0]]
        in_specs += [held, pl.BlockSpec(memory_space=pl.ANY)]
        aliases = {n + 3: 1, n + 4: 0}
    return pl.pallas_call(
        functools.partial(panel_kernel, places, first),
        grid=(size // tile,),
        in_specs=in_specs,
        out_specs=[tiled, held],
        out_shape=[jax.ShapeDtypeStruct((rows, cols), F32), pltpu.VMEM((depth, cols), F32)],
        input_output_aliases=aliases,
        scratch_shapes=[pltpu.VMEM((depth, tile), BF16)] * 2 + [pltpu.VMEM((depth, cols), BF16)] * 2,
        compiler_params=pltpu.CompilerParams(vmem_limit_bytes=VMEM_BYTES),
        cost_estimate=pl.CostEstimate(
            flops=18 * size * depth * cols, bytes_accessed=12 * size * cols, transcendentals=0
        ),
    )(*args)


def cut(rows):
    tile = 256
    while rows % tile or rows // tile < 14:
        tile //= 2
    tiles = rows // tile
    part = tiles // 14
    sizes = [part, 4 * part, 4 * part, tiles - 11 * part, 2 * part]
    return [s * tile for s in sizes], tile


def after(x, *done):
    return lax.optimization_barrier((x, *done))[0] if done else x


def local(panel_adj, inv_diag, row_panel, trailing_adj, trailing_factor):
    n_row, n_col = lax.axis_size("row"), lax.axis_size("col")
    rows, kb = panel_adj.shape
    depth = kb * n_col
    planes = n_col // 4
    pairs = dict(
        x=[(c, c ^ 1) for c in range(n_col)],
        y=[(c, c ^ 2) for c in range(n_col)],
        up=[(c, (c + 4) % n_col) for c in range(n_col)],
        down=[(c, (c - 4) % n_col) for c in range(n_col)],
    )

    def send(way, x, *done):
        return lax.ppermute(after(x, *done), "col", pairs[way])

    def over_row(x, *done):
        if n_row == 2:
            return x + lax.ppermute(after(x, *done), "row", [(0, 1), (1, 0)])
        return lax.psum(x, "row")

    def cross(block, *done):
        block = after(block, *done)
        return send("x", block), send("y", block)

    def corner(x, y, *done):
        x, y = lax.optimization_barrier((x, y, *done))[:2]
        half = x.shape[0] // 2
        return send("x", y[:half]), send("y", x[half:])

    def along_z(block, *done):
        block = after(block, *done)
        return [block] + [
            lax.ppermute(block, "col", [(c, (c + 4 * j) % n_col) for c in range(n_col)]) for j in range(1, planes)
        ]

    own = panel_adj.T
    share = depth // n_row
    inv_own = lax.dynamic_slice(inv_diag, (0, lax.axis_index("row") * share), (kb, share))
    sizes, tile = cut(rows)
    starts = [sum(sizes[:i]) for i in range(len(sizes))]
    chunk = [own[:, a : a + n] for a, n in zip(starts, sizes)]
    n1 = sizes[0]
    chunk[0] = jnp.concatenate([chunk[0], inv_own], 1)
    wide1 = chunk[0].shape[1]

    def near(block, *done):
        return send("up", block, *done), send("down", block, *done)

    def far(block, up, down, *done):
        got = [block, up]
        while len(got) < planes - 1:
            got.append(send("up", got[-1], *done))
        return [*got, down]

    early = jnp.concatenate([chunk[0], chunk[4]], 1)
    z1 = along_z(chunk[0])
    x0, y0 = cross(early)
    xy0 = corner(x0, y0)
    z2 = along_z(chunk[1], x0, y0, *z1)
    rest1 = jnp.concatenate(z1[1:], 0)
    x1, y1 = cross(rest1, *xy0)
    d2 = jnp.concatenate(z2, 0)
    xy1 = corner(x1, y1)
    x2, y2 = cross(d2, x1, y1)
    z3 = along_z(chunk[2], *xy1)

    wide = kb * planes
    hk, hw, hr = kb // 2, wide // 2, (wide - kb) // 2
    z_places = [[(0, wide, 0)], [(0, wide, wide)], [(0, wide, 2 * wide)], [(0, hw, 3 * wide)], [(0, hw, 3 * wide + hw)]]
    p_places = [[(kb * q, kb, wide * q + kb * j) for q in range(4)] for j in range(planes)]
    first_places = [[(0, kb, 0)], [(0, kb, wide)], [(0, kb, 2 * wide)], [(0, hk, 3 * wide)], [(0, hk, 3 * wide + hk)],
                    [(0, wide - kb, kb)], [(0, wide - kb, wide + kb)], [(0, wide - kb, 2 * wide + kb)],
                    [(0, hr, 3 * wide + kb)], [(0, hr, 3 * wide + kb + hr)]]
    first = [p[:, :wide1] for p in (early, x0, y0, *xy0)] + [rest1, x1, y1, *xy1]
    inverse = jnp.concatenate([first[i][:, n1:] for i in (0, 5, 1, 6, 2, 7, 3, 4, 8, 9)], 0)
    w = over_row(jnp.dot(inverse, row_panel, precision=HIGHEST, preferred_element_type=F32))
    step = functools.partial(panel_step, [], factor=trailing_factor, adj=trailing_adj, w=w, tile=tile)

    def halves(got, state, c):
        size = sizes[c] // (2 * tile) * tile
        half = step(got, z_places, state=state, start=starts[c], skip=0, size=size)
        rest = sizes[c] - size
        return half, step(got, z_places, state=half, start=starts[c] + size, skip=size, size=rest)

    s1 = step(first, first_places, state=None, start=starts[0], skip=0, size=sizes[0])
    xy2 = corner(x2, y2, s1[1])
    d3 = jnp.concatenate(z3, 0)
    x3, y3 = cross(d3, x2, y2, s1[1])
    z4 = along_z(chunk[3], *xy2)
    s2a, s2 = halves([d2, x2, y2, *xy2], s1, 1)
    xy3 = corner(x3, y3, s2a[1])
    d4 = jnp.concatenate(z4, 0)
    x4, y4 = cross(d4, x3, y3, s2a[1])
    plane = jnp.concatenate([p[:, wide1:] for p in (early, x0, y0, *xy0)], 0)
    z5 = near(plane, z4[2], s2a[1])
    s3a, s3 = halves([d3, x3, y3, *xy3], s2, 2)
    xy4 = corner(x4, y4, s3a[1])
    z5 = far(plane, *z5, s3a[1])
    s5 = step(z5, p_places, state=s3, start=starts[4], skip=0, size=sizes[4])
    out, sums = step([d4, x4, y4, *xy4], z_places, state=s5, start=starts[3], skip=0, size=sizes[3])
    row_adj = lax.dot_general(
        inverse, over_row(sums), (((0,), (0,)), ((), ())), precision=HIGHEST, preferred_element_type=F32
    )
    return out, row_adj


def solution(mesh):
    placed = (P("row", "col"), P("col", None), P("row", "col"), P("row", "col"), P("row", "col"))
    return jax.shard_map(
        local,
        mesh=mesh,
        in_specs=placed,
        out_specs=(P("row", "col"), P("row", "col")),
        check_vma=False,
    )
```

time: 433 us -> 183 us (0.42)
  waiting for transfers between devices: 231 us -> 52.3 us
  matrix products: 179 us -> 4.65 us
  Pallas kernels: 0 us -> 71.9 us
  starting transfers between devices: 0.15 us -> 47.1 us
  between operations: 13.8 us -> 1.05 us
    all_gather x3 -> x0, waiting for transfers between devices: 229 us -> none  [the longest x1 173 us: local(): lax.all_gather(panel_adj, 'col', axis=1, tiled=True)]
    dot_general x3 -> x2, matrix products: 179 us -> 4.65 us  [the longest x1 2.81 us: local(): lax.dot_general(inverse, over_row(sums), (((0,), (0,)), ((), ())), precis...]
    pallas_call x0 -> x7, Pallas kernels: none -> 71.9 us  [panel_step(): pl.pallas_call(functools.partial(panel_kernel, places, first), grid=(size...]
    ppermute x0 -> x37, waiting for transfers between devices: none -> 52.3 us  [the longest x23 40.2 us: send(): return lax.ppermute(after(x, *done), 'col', pairs[way])]
    ppermute x0 -> x37, starting transfers between devices: none -> 47.1 us  [the longest x23 20 us: send(): return lax.ppermute(after(x, *done), 'col', pairs[way])]
  transfers between devices with their start and end apart: 4 -> 37, of which waited for: 2 -> 17; matrix products, arithmetic and copies ran while one was open for 42% -> 3% of each run, Pallas kernels for 0% -> 32%
where the time goes in v1:
time: 183 us; the launch traced here: 182 us
  Pallas kernels  71.9 us (39%)
  waiting for transfers between devices  52.3 us (29%)
  starting transfers between devices  47.1 us (26%)
  local copies, waits for them, and re-layouts  5.22 us (3%)
  matrix products  4.65 us (3%)
    pallas_call x7, Pallas kernels, panel_step(): pl.pallas_call(functools.partial(panel_kernel, places, first), grid=(size...  71.9 us
    ppermute x23, waiting for transfers between devices, send(): return lax.ppermute(after(x, *done), 'col', pairs[way])  40.2 us
    ppermute x23, starting transfers between devices, send(): return lax.ppermute(after(x, *done), 'col', pairs[way])  20 us
    ppermute x2, starting transfers between devices, over_row(): return x + lax.ppermute(after(x, *done), 'row', [(0, 1), (1, 0)])  18.1 us
    ppermute x12, starting transfers between devices, along_z(): lax.ppermute(block, 'col', [(c, (c + 4 * j) % n_col) for c in range(n_col)])  9 us
    ppermute x12, waiting for transfers between devices, along_z(): lax.ppermute(block, 'col', [(c, (c + 4 * j) % n_col) for c in range(n_col)])  8.69 us
  transfers between devices with their start and end apart: 37, of which 17 were waited for; matrix products, arithmetic and copies ran while one was open for 3% of the time, Pallas kernels for 32%

profile of v1, /device:TPU:13, one launch (start us, length us, event | category | flops | bytes accessed | tf_op | source)
XLA Modules:
  0.0 182.4 jit_solution(15340402128239822678)
XLA Ops:
  0.7 0.9 slice.134
  1.6 0.8 constant_dynamic-update-slice_fusion.13
  2.4 1.3 collective-permute-start.2
  3.7 1.1 collective-permute-start.3
  4.8 1.4 collective-permute-start.4
  6.2 0.9 constant_dynamic-update-slice_fusion.22
  7.1 1.3 collective-permute-start
  8.6 1.1 fusion.2
  9.7 0.9 slice.132
  10.7 0.9 collective-permute-done.3
  11.6 2.7 %collective-permute-done.4 = f32[32,768]{1,0:T(8,128)S(1)} collective-permute-done((f32[32,768]{1,0:T(8,128)S(1)}, f32[32,768]{1,0:T(8,128)S(1)}, u32[]{:S(2)}, u32[]{:S(2)}) %collective-permute-start.4) | collective-permute-done | bytes 98336 | tf_op jit(solution)/shard_map/ppermute | solution.py:128
  14.4 1.3 collective-permute-start.8
  16.0 1.5 collective-permute-start.6
  18.1 1.6 collective-permute-done.9
  20.2 5.8 %collective-permute-done.10.refs_6_ = f32[96,768]{1,0:T(8,128)S(1)} collective-permute-done((f32[96,768]{1,0:T(8,128)S(1)}, f32[96,768]{1,0:T(8,128)S(1)}, u32[]{:S(2)}, u32[]{:S(2)}) %collective-permute-start.10) | collective-permute-done | bytes 294944 | tf_op jit(solution)/shard_map/ppermute | solution.py:109
  26.0 1.2 collective-permute-start.14
  27.5 2.9 %collective-permute-done.14.refs_8_ = f32[48,768]{1,0:T(8,128)S(1)} collective-permute-done((f32[48,768]{1,0:T(8,128)S(1)}, f32[48,768]{1,0:T(8,128)S(1)}, u32[]{:S(2)}, u32[]{:S(2)}) %collective-permute-start.14) | collective-permute-done | bytes 147488 | tf_op jit(solution)/shard_map/ppermute | solution.py:109
  30.3 1.3 collective-permute-done.15.refs_9_
  31.6 1.8 %fusion.3 = f32[512,896]{1,0:T(8,128)S(1)} fusion(f32[512,256]{1,0:T(8,128)S(1)} %constant_dynamic-update-slice_fusion.7, f32[256,896]{1,0:T(8,128)S(1)} %copy-done), kind=kOutput, calls=%fused_computation.36 | convolution fusion | flops 1409286144 | bytes 3276800 | tf_op jit(solution)/shard_map/dot_general | solution.py:171
  33.4 4.6 %collective-permute-start.16 = (f32[512,896]{1,0:T(8,128)S(1)}, f32[512,896]{1,0:T(8,128)S(1)}, u32[]{:S(2)}, u32[]{:S(2)}) collective-permute-start(f32[512,896]{1,0:T(8,128)S(1)} %fusion.3), channel_id=1, source_target_pairs={{0,16},{16,0},{1,17},{17,1},{2,18},{18,2},{3,19},{19,3},{4,20},{20... | collective-permute-start | bytes 5505032 | tf_op jit(solution)/shard_map/ppermute | solution.py:113
  38.3 3.0 %collective-permute-done.7 = f32[32,2048]{1,0:T(8,128)S(1)} collective-permute-done((f32[32,2048]{1,0:T(8,128)S(1)}, f32[32,2048]{1,0:T(8,128)S(1)}, u32[]{:S(2)}, u32[]{:S(2)}) %collective-permute-start.7) | collective-permute-done | bytes 262176 | tf_op jit(solution)/shard_map/ppermute | solution.py:128
  41.3 1.2 collective-permute-start.12
  42.6 1.2 collective-permute-start.13
  44.0 1.4 collective-permute-start.24
  45.6 6.6 %shard_map.68 = (f32[7168,896]{1,0:T(8,128)}, f32[512,896]{1,0:T(8,128)S(1)}) custom-call(f32[32,768]{1,0:T(8,128)S(1)} %pad_maximum_fusion.1.refs_0_, f32[32,768]{1,0:T(8,128)S(1)} %slice.136.refs_1_, f32[32,768]{1,0:T(8,128)S(1)} %slice.137.refs_2_, f32[16,768]{1,0:T(8,128)S(1)} %slice.138.refs_3_, f32[16,768]{1,0:T(8,128)S(1)} %slice.139.refs_4_, ...), custom_call_target="tpu_custom_call" | custom-call | flops 4227858432 | bytes 5505024 | tf_op jit(solution)/shard_map/pallas_call | solution.py:67
  52.2 13.4 %collective-permute-done.12.refs_1_ = f32[128,2048]{1,0:T(8,128)S(1)} collective-permute-done((f32[128,2048]{1,0:T(8,128)S(1)}, f32[128,2048]{1,0:T(8,128)S(1)}, u32[]{:S(2)}, u32[]{:S(2)}) %collective-permute-start.12) | collective-permute-done | bytes 1048608 | tf_op jit(solution)/shard_map/ppermute | solution.py:109
  65.6 0.9 collective-permute-done.13.refs_2_
  66.9 1.3 collective-permute-start.18
  68.3 1.2 collective-permute-start.25
  69.8 8.6 %collective-permute-done.17.refs_3_ = f32[64,2048]{1,0:T(8,128)S(1)} collective-permute-done((f32[64,2048]{1,0:T(8,128)S(1)}, f32[64,2048]{1,0:T(8,128)S(1)}, u32[]{:S(2)}, u32[]{:S(2)}) %collective-permute-start.17) | collective-permute-done | bytes 524320 | tf_op jit(solution)/shard_map/ppermute | solution.py:109
  78.5 1.2 collective-permute-start.19
  79.7 0.9 collective-permute-start.21
  80.5 10.2 %shard_map.69 = (f32[7168,896]{1,0:T(8,128)}, f32[512,896]{1,0:T(8,128)S(1)}) custom-call(f32[128,2048]{1,0:T(8,128)S(1)} %constant_dynamic-update-slice_fusion.refs_0_, f32[128,2048]{1,0:T(8,128)S(1)} %collective-permute-done.12.refs_1_, f32[128,2048]{1,0:T(8,128)S(1)} %collective-permute-done.13.refs_2_, ...), custom_call_target="tpu_custom_call", output_to_operand_aliasing={{1}: (8, {}), {0}: (9, {})} | custom-call | flops 8455716864 | bytes 11010048 | tf_op jit(solution)/shard_map/pallas_call | solution.py:67
  91.5 2.9 %collective-permute-start.35 = (f32[128,1024]{1,0:T(8,128)S(1)}, f32[128,1024]{1,0:T(8,128)S(1)}, u32[]{:S(2)}, u32[]{:S(2)}) collective-permute-start(f32[128,1024]{1,0:T(8,128)S(1)} %slice_dynamic-update-slice_fusion.5.refs_0_), channel_id=1, source_target_pairs={{0,12},{1,13},{2,14},{3,15},{4,0},{5,1},{6,2},{7,3},{8,4},{9,5},{1... | collective-permute-start | bytes 1572872 | tf_op jit(solution)/shard_map/ppermute | solution.py:109
  94.4 2.0 %collective-permute-done.21 = f32[32,1536]{1,0:T(8,128)S(1)} collective-permute-done((f32[32,1536]{1,0:T(8,128)S(1)}, f32[32,1536]{1,0:T(8,128)S(1)}, u32[]{:S(2)}, u32[]{:S(2)}) %collective-permute-start.21) | collective-permute-done | bytes 196640 | tf_op jit(solution)/shard_map/ppermute | solution.py:128
  96.4 4.4 %collective-permute-done.25.refs_1_ = f32[128,2048]{1,0:T(8,128)S(1)} collective-permute-done((f32[128,2048]{1,0:T(8,128)S(1)}, f32[128,2048]{1,0:T(8,128)S(1)}, u32[]{:S(2)}, u32[]{:S(2)}) %collective-permute-start.25) | collective-permute-done | bytes 1048608 | tf_op jit(solution)/shard_map/ppermute | solution.py:109
  101.0 1.2 collective-permute-start.29
  102.2 1.3 collective-permute-start.30
  103.9 10.2 %shard_map.70 = (f32[7168,896]{1,0:T(8,128)}, f32[512,896]{1,0:T(8,128)S(1)}) custom-call(f32[128,2048]{1,0:T(8,128)S(1)} %constant_dynamic-update-slice_fusion.refs_0_, f32[128,2048]{1,0:T(8,128)S(1)} %collective-permute-done.12.refs_1_, f32[128,2048]{1,0:T(8,128)S(1)} %collective-permute-done.13.refs_2_, ...), custom_call_target="tpu_custom_call", output_to_operand_aliasing={{1}: (8, {}), {0}: (9, {})} | custom-call | flops 8455716864 | bytes 11010048 | tf_op jit(solution)/shard_map/pallas_call | solution.py:67
  114.4 10.2 %shard_map.71 = (f32[7168,896]{1,0:T(8,128)}, f32[512,896]{1,0:T(8,128)S(1)}) custom-call(f32[128,2048]{1,0:T(8,128)S(1)} %constant_dynamic-update-slice_fusion.18.refs_0_, f32[128,2048]{1,0:T(8,128)S(1)} %collective-permute-done.25.refs_1_, f32[128,2048]{1,0:T(8,128)S(1)} %collective-permute-done.26.refs_2_, ...), custom_call_target="tpu_custom_call", output_to_operand_aliasing={{1}: (8, {}), {0}: (9, {})} | custom-call | flops 8455716864 | bytes 11010048 | tf_op jit(solution)/shard_map/pallas_call | solution.py:67
  124.6 0.8 collective-permute-start.34
  126.8 1.3 collective-permute-start.32
  128.1 10.2 %shard_map.72 = (f32[7168,896]{1,0:T(8,128)}, f32[512,896]{1,0:T(8,128)S(1)}) custom-call(f32[128,2048]{1,0:T(8,128)S(1)} %constant_dynamic-update-slice_fusion.18.refs_0_, f32[128,2048]{1,0:T(8,128)S(1)} %collective-permute-done.25.refs_1_, f32[128,2048]{1,0:T(8,128)S(1)} %collective-permute-done.26.refs_2_, ...), custom_call_target="tpu_custom_call", output_to_operand_aliasing={{1}: (8, {}), {0}: (9, {})} | custom-call | flops 8455716864 | bytes 11010048 | tf_op jit(solution)/shard_map/pallas_call | solution.py:67
  138.3 10.2 %shard_map.73 = (f32[7168,896]{1,0:T(8,128)}, f32[512,896]{1,0:T(8,128)S(1)}) custom-call(f32[128,1024]{1,0:T(8,128)S(1)} %slice_dynamic-update-slice_fusion.5.refs_0_, f32[128,1024]{1,0:T(8,128)S(1)} %collective-permute-done.33.refs_1_, f32[128,1024]{1,0:T(8,128)S(1)} %collective-permute-done.34.refs_2_, ...), custom_call_target="tpu_custom_call", output_to_operand_aliasing={{1}: (7, {}), {0}: (8, {})} | custom-call | flops 8455716864 | bytes 11010048 | tf_op jit(solution)/shard_map/pallas_call | solution.py:67
  148.6 14.2 %shard_map.74 = (f32[7168,896]{1,0:T(8,128)}, f32[512,896]{1,0:T(8,128)S(1)}) custom-call(f32[128,1536]{1,0:T(8,128)S(1)} %constant_dynamic-update-slice_fusion.14.refs_0_, f32[128,1536]{1,0:T(8,128)S(1)} %collective-permute-done.27.refs_1_, f32[128,1536]{1,0:T(8,128)S(1)} %collective-permute-done.28.refs_2_, ...), custom_call_target="tpu_custom_call", output_to_operand_aliasing={{1}: (8, {}), {0}: (9, {})} | custom-call | flops 12683575296 | bytes 16515072 | tf_op jit(solution)/shard_map/pallas_call | solution.py:67
  162.7 13.4 %collective-permute-start.36 = (f32[512,896]{1,0:T(8,128)S(1)}, f32[512,896]{1,0:T(8,128)S(1)}, u32[]{:S(2)}, u32[]{:S(2)}) collective-permute-start(f32[512,896]{1,0:T(8,128)S(1)} %get-tuple-element.67), channel_id=1, source_target_pairs={{0,16},{16,0},{1,17},{17,1},{2,18},{18,2},{3,19},{19,3},{4,20},{20... | collective-permute-start | bytes 5505032 | tf_op jit(solution)/shard_map/ppermute | solution.py:113
  176.2 3.4 %collective-permute-done.36 = f32[512,896]{1,0:T(8,128)S(1)} collective-permute-done((f32[512,896]{1,0:T(8,128)S(1)}, f32[512,896]{1,0:T(8,128)S(1)}, u32[]{:S(2)}, u32[]{:S(2)}) %collective-permute-start.36) | collective-permute-done | bytes 1835040 | tf_op jit(solution)/shard_map/ppermute | solution.py:113
  179.6 2.8 %fusion = f32[256,896]{1,0:T(8,128)} fusion(f32[512,256]{1,0:T(8,128)S(1)} %copy-done.3, f32[512,896]{1,0:T(8,128)S(1)} %get-tuple-element.67, f32[512,896]{1,0:T(8,128)S(1)} %collective-permute-done.36), kind=kOutput, calls=%fused_computation | convolution fusion | flops 1409744896 | bytes 5111808 | tf_op jit(solution)/shard_map/dot_general | solution.py:196
  (93 shorter events, 6.3 us)
Async XLA Ops:
  0.6 31.0 %copy-start = (f32[256,896]{1,0:T(8,128)S(1)}, f32[256,896]{1,0:T(8,128)}, u32[]{:S(2)}) copy-start(f32[256,896]{1,0:T(8,128)} %param.7) | copy-start | bytes 2752516
  2.4 8.3 %collective-permute-start.2 = (f32[32,768]{1,0:T(8,128)S(1)}, f32[32,768]{1,0:T(8,128)S(1)}, u32[]{:S(2)}, u32[]{:S(2)}) collective-permute-start(f32[32,768]{1,0:T(8,128)S(1)} %pad_maximum_fusion.1.refs_0_), channel_id=1, source_target_pairs={{0,4},{1,5},{2,6},{3,7},{4,8},{5,9},{6,10},{7,11},{8,12},{9,13},{1... | collective-permute-start | bytes 294920 | tf_op jit(solution)/shard_map/ppermute | solution.py:128
  3.7 7.9 %collective-permute-start.3 = (f32[32,768]{1,0:T(8,128)S(1)}, f32[32,768]{1,0:T(8,128)S(1)}, u32[]{:S(2)}, u32[]{:S(2)}) collective-permute-start(f32[32,768]{1,0:T(8,128)S(1)} %pad_maximum_fusion.1.refs_0_), channel_id=1, source_target_pairs={{0,8},{1,9},{2,10},{3,11},{4,12},{5,13},{6,14},{7,15},{8,0},{9,1},... | collective-permute-start | bytes 294920 | tf_op jit(solution)/shard_map/ppermute | solution.py:128
  4.8 9.5 %collective-permute-start.4 = (f32[32,768]{1,0:T(8,128)S(1)}, f32[32,768]{1,0:T(8,128)S(1)}, u32[]{:S(2)}, u32[]{:S(2)}) collective-permute-start(f32[32,768]{1,0:T(8,128)S(1)} %pad_maximum_fusion.1.refs_0_), channel_id=1, source_target_pairs={{0,12},{1,13},{2,14},{3,15},{4,0},{5,1},{6,2},{7,3},{8,4},{9,5},{1... | collective-permute-start | bytes 294920 | tf_op jit(solution)/shard_map/ppermute | solution.py:128
  7.1 7.2 %collective-permute-start = (f32[32,1792]{1,0:T(8,128)S(1)}, f32[32,1792]{1,0:T(8,128)S(1)}, u32[]{:S(2)}, u32[]{:S(2)}) collective-permute-start(f32[32,1792]{1,0:T(8,128)S(1)} %pad_maximum_fusion), channel_id=1, source_target_pairs={{0,1},{1,0},{2,3},{3,2},{4,5},{5,4},{6,7},{7,6},{8,9},{9,8},{10,11... | collective-permute-start | bytes 688136 | tf_op jit(solution)/shard_map/ppermute | solution.py:109
  8.4 6.0 %collective-permute-start.1 = (f32[32,1792]{1,0:T(8,128)S(1)}, f32[32,1792]{1,0:T(8,128)S(1)}, u32[]{:S(2)}, u32[]{:S(2)}) collective-permute-start(f32[32,1792]{1,0:T(8,128)S(1)} %pad_maximum_fusion), channel_id=1, source_target_pairs={{0,2},{1,3},{2,0},{3,1},{4,6},{5,7},{6,4},{7,5},{8,10},{9,11},{10,... | collective-permute-start | bytes 688136 | tf_op jit(solution)/shard_map/ppermute | solution.py:109
  14.4 3.7 %collective-permute-start.8 = (f32[16,1792]{1,0:T(8,128)S(1)}, f32[16,1792]{1,0:T(8,128)S(1)}, u32[]{:S(2)}, u32[]{:S(2)}) collective-permute-start(f32[16,1792]{1,0:T(8,128)S(1)} %slice.104), channel_id=1, source_target_pairs={{0,1},{1,0},{2,3},{3,2},{4,5},{5,4},{6,7},{7,6},{8,9},{9,8},{10,11... | collective-permute-start | bytes 344072 | tf_op jit(solution)/shard_map/ppermute | solution.py:109
  15.7 4.0 %collective-permute-start.9 = (f32[16,1792]{1,0:T(8,128)S(1)}, f32[16,1792]{1,0:T(8,128)S(1)}, u32[]{:S(2)}, u32[]{:S(2)}) collective-permute-start(f32[16,1792]{1,0:T(8,128)S(1)} %slice.105), channel_id=1, source_target_pairs={{0,2},{1,3},{2,0},{3,1},{4,6},{5,7},{6,4},{7,5},{8,10},{9,11},{10,... | collective-permute-start | bytes 344072 | tf_op jit(solution)/shard_map/ppermute | solution.py:109
  16.0 22.2 %collective-permute-start.5 = (f32[32,2048]{1,0:T(8,128)S(1)}, f32[32,2048]{1,0:T(8,128)S(1)}, u32[]{:S(2)}, u32[]{:S(2)}) collective-permute-start(f32[32,2048]{1,0:T(8,128)S(1)} %get-tuple-element.35), channel_id=1, source_target_pairs={{0,4},{1,5},{2,6},{3,7},{4,8},{5,9},{6,10},{7,11},{8,12},{9,13},{1... | collective-permute-start | bytes 786440 | tf_op jit(solution)/shard_map/ppermute | solution.py:128
  16.0 22.2 %collective-permute-start.6 = (f32[32,2048]{1,0:T(8,128)S(1)}, f32[32,2048]{1,0:T(8,128)S(1)}, u32[]{:S(2)}, u32[]{:S(2)}) collective-permute-start(f32[32,2048]{1,0:T(8,128)S(1)} %get-tuple-element.35), channel_id=1, source_target_pairs={{0,8},{1,9},{2,10},{3,11},{4,12},{5,13},{6,14},{7,15},{8,0},{9,1},... | collective-permute-start | bytes 786440 | tf_op jit(solution)/shard_map/ppermute | solution.py:128
  17.6 23.7 %collective-permute-start.7 = (f32[32,2048]{1,0:T(8,128)S(1)}, f32[32,2048]{1,0:T(8,128)S(1)}, u32[]{:S(2)}, u32[]{:S(2)}) collective-permute-start(f32[32,2048]{1,0:T(8,128)S(1)} %get-tuple-element.35), channel_id=1, source_target_pairs={{0,12},{1,13},{2,14},{3,15},{4,0},{5,1},{6,2},{7,3},{8,4},{9,5},{1... | collective-permute-start | bytes 786440 | tf_op jit(solution)/shard_map/ppermute | solution.py:128
  19.7 6.3 %collective-permute-start.10 = (f32[96,768]{1,0:T(8,128)S(1)}, f32[96,768]{1,0:T(8,128)S(1)}, u32[]{:S(2)}, u32[]{:S(2)}) collective-permute-start(f32[96,768]{1,0:T(8,128)S(1)} %constant_dynamic-update-slice_fusion.4.refs_5_), channel_id=1, source_target_pairs={{0,1},{1,0},{2,3},{3,2},{4,5},{5,4},{6,7},{7,6},{8,9},{9,8},{10,11... | collective-permute-start | bytes 884744 | tf_op jit(solution)/shard_map/ppermute | solution.py:109
  19.9 6.0 %collective-permute-start.11 = (f32[96,768]{1,0:T(8,128)S(1)}, f32[96,768]{1,0:T(8,128)S(1)}, u32[]{:S(2)}, u32[]{:S(2)}) collective-permute-start(f32[96,768]{1,0:T(8,128)S(1)} %constant_dynamic-update-slice_fusion.4.refs_5_), channel_id=1, source_target_pairs={{0,2},{1,3},{2,0},{3,1},{4,6},{5,7},{6,4},{7,5},{8,10},{9,11},{10,... | collective-permute-start | bytes 884744 | tf_op jit(solution)/shard_map/ppermute | solution.py:109
  26.0 4.4 %collective-permute-start.14 = (f32[48,768]{1,0:T(8,128)S(1)}, f32[48,768]{1,0:T(8,128)S(1)}, u32[]{:S(2)}, u32[]{:S(2)}) collective-permute-start(f32[48,768]{1,0:T(8,128)S(1)} %slice.110), channel_id=1, source_target_pairs={{0,1},{1,0},{2,3},{3,2},{4,5},{5,4},{6,7},{7,6},{8,9},{9,8},{10,11... | collective-permute-start | bytes 442376 | tf_op jit(solution)/shard_map/ppermute | solution.py:109
  27.2 4.4 %collective-permute-start.15 = (f32[48,768]{1,0:T(8,128)S(1)}, f32[48,768]{1,0:T(8,128)S(1)}, u32[]{:S(2)}, u32[]{:S(2)}) collective-permute-start(f32[48,768]{1,0:T(8,128)S(1)} %slice.111), channel_id=1, source_target_pairs={{0,2},{1,3},{2,0},{3,1},{4,6},{5,7},{6,4},{7,5},{8,10},{9,11},{10,... | collective-permute-start | bytes 442376 | tf_op jit(solution)/shard_map/ppermute | solution.py:109
  31.6 6.5 %copy-start.2 = (f32[512,256]{1,0:T(8,128)}, f32[512,256]{1,0:T(8,128)S(1)}, u32[]{:S(2)}) copy-start(f32[512,256]{1,0:T(8,128)S(1)} %constant_dynamic-update-slice_fusion.7) | copy-start | bytes 1572868
  33.4 10.5 %collective-permute-start.16 = (f32[512,896]{1,0:T(8,128)S(1)}, f32[512,896]{1,0:T(8,128)S(1)}, u32[]{:S(2)}, u32[]{:S(2)}) collective-permute-start(f32[512,896]{1,0:T(8,128)S(1)} %fusion.3), channel_id=1, source_target_pairs={{0,16},{16,0},{1,17},{17,1},{2,18},{18,2},{3,19},{19,3},{4,20},{20... | collective-permute-start | bytes 5505032 | tf_op jit(solution)/shard_map/ppermute | solution.py:113
  41.3 24.3 %collective-permute-start.12 = (f32[128,2048]{1,0:T(8,128)S(1)}, f32[128,2048]{1,0:T(8,128)S(1)}, u32[]{:S(2)}, u32[]{:S(2)}) collective-permute-start(f32[128,2048]{1,0:T(8,128)S(1)} %constant_dynamic-update-slice_fusion.refs_0_), channel_id=1, source_target_pairs={{0,1},{1,0},{2,3},{3,2},{4,5},{5,4},{6,7},{7,6},{8,9},{9,8},{10,11... | collective-permute-start | bytes 3145736 | tf_op jit(solution)/shard_map/ppermute | solution.py:109
  42.6 23.9 %collective-permute-start.13 = (f32[128,2048]{1,0:T(8,128)S(1)}, f32[128,2048]{1,0:T(8,128)S(1)}, u32[]{:S(2)}, u32[]{:S(2)}) collective-permute-start(f32[128,2048]{1,0:T(8,128)S(1)} %constant_dynamic-update-slice_fusion.refs_0_), channel_id=1, source_target_pairs={{0,2},{1,3},{2,0},{3,1},{4,6},{5,7},{6,4},{7,5},{8,10},{9,11},{10,... | collective-permute-start | bytes 3145736 | tf_op jit(solution)/shard_map/ppermute | solution.py:109
  43.8 24.4 %collective-permute-start.22 = (f32[32,2048]{1,0:T(8,128)S(1)}, f32[32,2048]{1,0:T(8,128)S(1)}, u32[]{:S(2)}, u32[]{:S(2)}) collective-permute-start(f32[32,2048]{1,0:T(8,128)S(1)} %get-tuple-element.46), channel_id=1, source_target_pairs={{0,4},{1,5},{2,6},{3,7},{4,8},{5,9},{6,10},{7,11},{8,12},{9,13},{1... | collective-permute-start | bytes 786440 | tf_op jit(solution)/shard_map/ppermute | solution.py:128
  43.9 24.4 %collective-permute-start.23 = (f32[32,2048]{1,0:T(8,128)S(1)}, f32[32,2048]{1,0:T(8,128)S(1)}, u32[]{:S(2)}, u32[]{:S(2)}) collective-permute-start(f32[32,2048]{1,0:T(8,128)S(1)} %get-tuple-element.46), channel_id=1, source_target_pairs={{0,8},{1,9},{2,10},{3,11},{4,12},{5,13},{6,14},{7,15},{8,0},{9,1},... | collective-permute-start | bytes 786440 | tf_op jit(solution)/shard_map/ppermute | solution.py:128
  44.0 24.3 %collective-permute-start.24 = (f32[32,2048]{1,0:T(8,128)S(1)}, f32[32,2048]{1,0:T(8,128)S(1)}, u32[]{:S(2)}, u32[]{:S(2)}) collective-permute-start(f32[32,2048]{1,0:T(8,128)S(1)} %get-tuple-element.46), channel_id=1, source_target_pairs={{0,12},{1,13},{2,14},{3,15},{4,0},{5,1},{6,2},{7,3},{8,4},{9,5},{1... | collective-permute-start | bytes 786440 | tf_op jit(solution)/shard_map/ppermute | solution.py:128
  66.5 11.8 %collective-permute-start.17 = (f32[64,2048]{1,0:T(8,128)S(1)}, f32[64,2048]{1,0:T(8,128)S(1)}, u32[]{:S(2)}, u32[]{:S(2)}) collective-permute-start(f32[64,2048]{1,0:T(8,128)S(1)} %slice.121), channel_id=1, source_target_pairs={{0,1},{1,0},{2,3},{3,2},{4,5},{5,4},{6,7},{7,6},{8,9},{9,8},{10,11... | collective-permute-start | bytes 1572872 | tf_op jit(solution)/shard_map/ppermute | solution.py:109
  66.9 11.6 %collective-permute-start.18 = (f32[64,2048]{1,0:T(8,128)S(1)}, f32[64,2048]{1,0:T(8,128)S(1)}, u32[]{:S(2)}, u32[]{:S(2)}) collective-permute-start(f32[64,2048]{1,0:T(8,128)S(1)} %slice.122), channel_id=1, source_target_pairs={{0,2},{1,3},{2,0},{3,1},{4,6},{5,7},{6,4},{7,5},{8,10},{9,11},{10,... | collective-permute-start | bytes 1572872 | tf_op jit(solution)/shard_map/ppermute | solution.py:109
  68.3 32.5 %collective-permute-start.25 = (f32[128,2048]{1,0:T(8,128)S(1)}, f32[128,2048]{1,0:T(8,128)S(1)}, u32[]{:S(2)}, u32[]{:S(2)}) collective-permute-start(f32[128,2048]{1,0:T(8,128)S(1)} %constant_dynamic-update-slice_fusion.18.refs_0_), channel_id=1, source_target_pairs={{0,1},{1,0},{2,3},{3,2},{4,5},{5,4},{6,7},{7,6},{8,9},{9,8},{10,11... | collective-permute-start | bytes 3145736 | tf_op jit(solution)/shard_map/ppermute | solution.py:109
  69.5 31.4 %collective-permute-start.26 = (f32[128,2048]{1,0:T(8,128)S(1)}, f32[128,2048]{1,0:T(8,128)S(1)}, u32[]{:S(2)}, u32[]{:S(2)}) collective-permute-start(f32[128,2048]{1,0:T(8,128)S(1)} %constant_dynamic-update-slice_fusion.18.refs_0_), channel_id=1, source_target_pairs={{0,2},{1,3},{2,0},{3,1},{4,6},{5,7},{6,4},{7,5},{8,10},{9,11},{10,... | collective-permute-start | bytes 3145736 | tf_op jit(solution)/shard_map/ppermute | solution.py:109
  78.5 12.3 %collective-permute-start.20 = (f32[32,1536]{1,0:T(8,128)S(1)}, f32[32,1536]{1,0:T(8,128)S(1)}, u32[]{:S(2)}, u32[]{:S(2)}) collective-permute-start(f32[32,1536]{1,0:T(8,128)S(1)} %slice.132), channel_id=1, source_target_pairs={{0,8},{1,9},{2,10},{3,11},{4,12},{5,13},{6,14},{7,15},{8,0},{9,1},... | collective-permute-start | bytes 589832 | tf_op jit(solution)/shard_map/ppermute | solution.py:128
  78.5 13.0 %collective-permute-start.19 = (f32[32,1536]{1,0:T(8,128)S(1)}, f32[32,1536]{1,0:T(8,128)S(1)}, u32[]{:S(2)}, u32[]{:S(2)}) collective-permute-start(f32[32,1536]{1,0:T(8,128)S(1)} %slice.132), channel_id=1, source_target_pairs={{0,4},{1,5},{2,6},{3,7},{4,8},{5,9},{6,10},{7,11},{8,12},{9,13},{1... | collective-permute-start | bytes 589832 | tf_op jit(solution)/shard_map/ppermute | solution.py:128
  79.7 16.7 %collective-permute-start.21 = (f32[32,1536]{1,0:T(8,128)S(1)}, f32[32,1536]{1,0:T(8,128)S(1)}, u32[]{:S(2)}, u32[]{:S(2)}) collective-permute-start(f32[32,1536]{1,0:T(8,128)S(1)} %slice.132), channel_id=1, source_target_pairs={{0,12},{1,13},{2,14},{3,15},{4,0},{5,1},{6,2},{7,3},{8,4},{9,5},{1... | collective-permute-start | bytes 589832 | tf_op jit(solution)/shard_map/ppermute | solution.py:128
  90.8 33.8 %collective-permute-start.33 = (f32[128,1024]{1,0:T(8,128)S(1)}, f32[128,1024]{1,0:T(8,128)S(1)}, u32[]{:S(2)}, u32[]{:S(2)}) collective-permute-start(f32[128,1024]{1,0:T(8,128)S(1)} %slice_dynamic-update-slice_fusion.5.refs_0_), channel_id=1, source_target_pairs={{0,4},{1,5},{2,6},{3,7},{4,8},{5,9},{6,10},{7,11},{8,12},{9,13},{1... | collective-permute-start | bytes 1572872 | tf_op jit(solution)/shard_map/ppermute | solution.py:109
  91.5 46.8 %collective-permute-start.35 = (f32[128,1024]{1,0:T(8,128)S(1)}, f32[128,1024]{1,0:T(8,128)S(1)}, u32[]{:S(2)}, u32[]{:S(2)}) collective-permute-start(f32[128,1024]{1,0:T(8,128)S(1)} %slice_dynamic-update-slice_fusion.5.refs_0_), channel_id=1, source_target_pairs={{0,12},{1,13},{2,14},{3,15},{4,0},{5,1},{6,2},{7,3},{8,4},{9,5},{1... | collective-permute-start | bytes 1572872 | tf_op jit(solution)/shard_map/ppermute | solution.py:109
  101.0 13.1 %collective-permute-start.29 = (f32[64,2048]{1,0:T(8,128)S(1)}, f32[64,2048]{1,0:T(8,128)S(1)}, u32[]{:S(2)}, u32[]{:S(2)}) collective-permute-start(f32[64,2048]{1,0:T(8,128)S(1)} %slice.124), channel_id=1, source_target_pairs={{0,1},{1,0},{2,3},{3,2},{4,5},{5,4},{6,7},{7,6},{8,9},{9,8},{10,11... | collective-permute-start | bytes 1572872 | tf_op jit(solution)/shard_map/ppermute | solution.py:109
  102.2 12.2 %collective-permute-start.30 = (f32[64,2048]{1,0:T(8,128)S(1)}, f32[64,2048]{1,0:T(8,128)S(1)}, u32[]{:S(2)}, u32[]{:S(2)}) collective-permute-start(f32[64,2048]{1,0:T(8,128)S(1)} %slice.125), channel_id=1, source_target_pairs={{0,2},{1,3},{2,0},{3,1},{4,6},{5,7},{6,4},{7,5},{8,10},{9,11},{10,... | collective-permute-start | bytes 1572872 | tf_op jit(solution)/shard_map/ppermute | solution.py:109
  103.5 21.9 %collective-permute-start.27 = (f32[128,1536]{1,0:T(8,128)S(1)}, f32[128,1536]{1,0:T(8,128)S(1)}, u32[]{:S(2)}, u32[]{:S(2)}) collective-permute-start(f32[128,1536]{1,0:T(8,128)S(1)} %constant_dynamic-update-slice_fusion.14.refs_0_), channel_id=1, source_target_pairs={{0,1},{1,0},{2,3},{3,2},{4,5},{5,4},{6,7},{7,6},{8,9},{9,8},{10,11... | collective-permute-start | bytes 2359304 | tf_op jit(solution)/shard_map/ppermute | solution.py:109
  114.2 11.9 %collective-permute-start.28 = (f32[128,1536]{1,0:T(8,128)S(1)}, f32[128,1536]{1,0:T(8,128)S(1)}, u32[]{:S(2)}, u32[]{:S(2)}) collective-permute-start(f32[128,1536]{1,0:T(8,128)S(1)} %constant_dynamic-update-slice_fusion.14.refs_0_), channel_id=1, source_target_pairs={{0,2},{1,3},{2,0},{3,1},{4,6},{5,7},{6,4},{7,5},{8,10},{9,11},{10,... | collective-permute-start | bytes 2359304 | tf_op jit(solution)/shard_map/ppermute | solution.py:109
  124.6 13.7 %collective-permute-start.34 = (f32[128,1024]{1,0:T(8,128)S(1)}, f32[128,1024]{1,0:T(8,128)S(1)}, u32[]{:S(2)}, u32[]{:S(2)}) collective-permute-start(f32[128,1024]{1,0:T(8,128)S(1)} %collective-permute-done.33.refs_1_), channel_id=1, source_target_pairs={{0,4},{1,5},{2,6},{3,7},{4,8},{5,9},{6,10},{7,11},{8,12},{9,13},{1... | collective-permute-start | bytes 1572872 | tf_op jit(solution)/shard_map/ppermute | solution.py:109
  126.1 22.5 %collective-permute-start.31 = (f32[64,1536]{1,0:T(8,128)S(1)}, f32[64,1536]{1,0:T(8,128)S(1)}, u32[]{:S(2)}, u32[]{:S(2)}) collective-permute-start(f32[64,1536]{1,0:T(8,128)S(1)} %slice.126), channel_id=1, source_target_pairs={{0,1},{1,0},{2,3},{3,2},{4,5},{5,4},{6,7},{7,6},{8,9},{9,8},{10,11... | collective-permute-start | bytes 1179656 | tf_op jit(solution)/shard_map/ppermute | solution.py:109
  126.8 21.8 %collective-permute-start.32 = (f32[64,1536]{1,0:T(8,128)S(1)}, f32[64,1536]{1,0:T(8,128)S(1)}, u32[]{:S(2)}, u32[]{:S(2)}) collective-permute-start(f32[64,1536]{1,0:T(8,128)S(1)} %slice.127), channel_id=1, source_target_pairs={{0,2},{1,3},{2,0},{3,1},{4,6},{5,7},{6,4},{7,5},{8,10},{9,11},{10,... | collective-permute-start | bytes 1179656 | tf_op jit(solution)/shard_map/ppermute | solution.py:109
  148.6 31.0 %copy-start.3 = (f32[512,256]{1,0:T(8,128)S(1)}, f32[512,256]{1,0:T(8,128)}, u32[]{:S(2)}) copy-start(f32[512,256]{1,0:T(8,128)} %copy-done.2) | copy-start | bytes 1572868
  162.7 19.7 %copy-start.1 = (f32[256,896]{1,0:T(8,128)S(1)}, f32[256,896]{1,0:T(8,128)}, u32[]{:S(2)}) copy-start(f32[256,896]{1,0:T(8,128)} %param.7) | copy-start | bytes 2752516
  162.7 16.8 %collective-permute-start.36 = (f32[512,896]{1,0:T(8,128)S(1)}, f32[512,896]{1,0:T(8,128)S(1)}, u32[]{:S(2)}, u32[]{:S(2)}) collective-permute-start(f32[512,896]{1,0:T(8,128)S(1)} %get-tuple-element.67), channel_id=1, source_target_pairs={{0,16},{16,0},{1,17},{17,1},{2,18},{18,2},{3,19},{19,3},{4,20},{20... | collective-permute-start | bytes 5505032 | tf_op jit(solution)/shard_map/ppermute | solution.py:113

commit v2 on v1

--- a/solution.py
+++ b/solution.py
@@ -9,7 +9,7 @@
 
 F32, BF16 = jnp.float32, jnp.bfloat16
 VMEM_BYTES = 32 << 20
-HIGHEST = lax.Precision.HIGHEST
+HIGH = lax.Precision.HIGH
 
 
 def two_terms(x):
@@ -168,7 +168,7 @@
                     [(0, hr, 3 * wide + kb)], [(0, hr, 3 * wide + kb + hr)]]
     first = [p[:, :wide1] for p in (early, x0, y0, *xy0)] + [rest1, x1, y1, *xy1]
     inverse = jnp.concatenate([first[i][:, n1:] for i in (0, 5, 1, 6, 2, 7, 3, 4, 8, 9)], 0)
-    w = over_row(jnp.dot(inverse, row_panel, precision=HIGHEST, preferred_element_type=F32))
+    w = over_row(jnp.dot(inverse, row_panel, precision=HIGH, preferred_element_type=F32))
     step = functools.partial(panel_step, [], factor=trailing_factor, adj=trailing_adj, w=w, tile=tile)
 
     def halves(got, state, c):
@@ -190,11 +190,11 @@
     z5 = near(plane, z4[2], s2a[1])
     s3a, s3 = halves([d3, x3, y3, *xy3], s2, 2)
     xy4 = corner(x4, y4, s3a[1])
-    z5 = far(plane, *z5, s3a[1])
+    z5 = far(plane, *z5)
     s5 = step(z5, p_places, state=s3, start=starts[4], skip=0, size=sizes[4])
     out, sums = step([d4, x4, y4, *xy4], z_places, state=s5, start=starts[3], skip=0, size=sizes[3])
     row_adj = lax.dot_general(
-        inverse, over_row(sums), (((0,), (0,)), ((), ())), precision=HIGHEST, preferred_element_type=F32
+        inverse, over_row(sums), (((0,), (0,)), ((), ())), precision=HIGH, preferred_element_type=F32
     )
     return out, row_adj
 

time: 183 us -> 180 us (0.984)
  starting transfers between devices: 47.1 us -> 38.4 us
  waiting for transfers between devices: 52.3 us -> 59.3 us
    ppermute x2, starting transfers between devices: 18.1 us -> 9.25 us  [over_row(): return x + lax.ppermute(after(x, *done), 'row', [(0, 1), (1, 0)])]
    ppermute x23, waiting for transfers between devices: 40.2 us -> 45.1 us  [send(): return lax.ppermute(after(x, *done), 'col', pairs[way])]
    ppermute x12, waiting for transfers between devices: 8.69 us -> 10.8 us  [along_z(): lax.ppermute(block, 'col', [(c, (c + 4 * j) % n_col) for c in range(n_col)])]
  transfers between devices with their start and end apart: 37 -> 37, of which waited for: 17 -> 19; matrix products, arithmetic and copies ran while one was open for 3% -> 3% of each run, Pallas kernels for 32% -> 32%
where the time goes in v2:
time: 180 us; the launch traced here: 179 us
  Pallas kernels  71.9 us (40%)
  waiting for transfers between devices  59.3 us (33%)
  starting transfers between devices  38.4 us (21%)
  local copies, waits for them, and re-layouts  5.22 us (3%)
  matrix products  2.97 us (2%)
    pallas_call x7, Pallas kernels, panel_step(): pl.pallas_call(functools.partial(panel_kernel, places, first), grid=(size...  71.9 us
    ppermute x23, waiting for transfers between devices, send(): return lax.ppermute(after(x, *done), 'col', pairs[way])  45.1 us
    ppermute x23, starting transfers between devices, send(): return lax.ppermute(after(x, *done), 'col', pairs[way])  20.7 us
    ppermute x12, waiting for transfers between devices, along_z(): lax.ppermute(block, 'col', [(c, (c + 4 * j) % n_col) for c in range(n_col)])  10.8 us
    ppermute x2, starting transfers between devices, over_row(): return x + lax.ppermute(after(x, *done), 'row', [(0, 1), (1, 0)])  9.25 us
    ppermute x12, starting transfers between devices, along_z(): lax.ppermute(block, 'col', [(c, (c + 4 * j) % n_col) for c in range(n_col)])  8.45 us
  transfers between devices with their start and end apart: 37, of which 19 were waited for; matrix products, arithmetic and copies ran while one was open for 3% of the time, Pallas kernels for 32%

profile of v2, /device:TPU:13, one launch (start us, length us, event | category | flops | bytes accessed | tf_op | source)
XLA Modules:
  0.0 179.1 jit_solution(2268106069219452699)
XLA Ops:
  0.7 0.9 slice.134
  2.4 1.3 collective-permute-start.2
  3.7 1.1 collective-permute-start.3
  4.8 1.4 collective-permute-start.4
  7.1 1.3 collective-permute-start
  8.6 1.1 fusion.2
  9.7 0.9 slice.132
  11.6 2.7 %collective-permute-done.4 = f32[32,768]{1,0:T(8,128)S(1)} collective-permute-done((f32[32,768]{1,0:T(8,128)S(1)}, f32[32,768]{1,0:T(8,128)S(1)}, u32[]{:S(2)}, u32[]{:S(2)}) %collective-permute-start.4) | collective-permute-done | bytes 98336 | tf_op jit(solution)/shard_map/ppermute | solution.py:128
  14.4 1.3 collective-permute-start.8
  16.0 1.5 collective-permute-start.6
  18.1 1.6 collective-permute-done.9
  20.2 5.8 %collective-permute-done.10.refs_6_ = f32[96,768]{1,0:T(8,128)S(1)} collective-permute-done((f32[96,768]{1,0:T(8,128)S(1)}, f32[96,768]{1,0:T(8,128)S(1)}, u32[]{:S(2)}, u32[]{:S(2)}) %collective-permute-start.10) | collective-permute-done | bytes 294944 | tf_op jit(solution)/shard_map/ppermute | solution.py:109
  26.0 1.2 collective-permute-start.14
  27.5 2.9 %collective-permute-done.14.refs_8_ = f32[48,768]{1,0:T(8,128)S(1)} collective-permute-done((f32[48,768]{1,0:T(8,128)S(1)}, f32[48,768]{1,0:T(8,128)S(1)}, u32[]{:S(2)}, u32[]{:S(2)}) %collective-permute-start.14) | collective-permute-done | bytes 147488 | tf_op jit(solution)/shard_map/ppermute | solution.py:109
  30.3 1.3 collective-permute-done.15.refs_9_
  31.6 1.0 fusion.3
  32.6 4.6 %collective-permute-start.16 = (f32[512,896]{1,0:T(8,128)S(1)}, f32[512,896]{1,0:T(8,128)S(1)}, u32[]{:S(2)}, u32[]{:S(2)}) collective-permute-start(f32[512,896]{1,0:T(8,128)S(1)} %fusion.3), channel_id=1, source_target_pairs={{0,16},{16,0},{1,17},{17,1},{2,18},{18,2},{3,19},{19,3},{4,20},{20... | collective-permute-start | bytes 5505032 | tf_op jit(solution)/shard_map/ppermute | solution.py:113
  37.4 3.9 %collective-permute-done.7 = f32[32,2048]{1,0:T(8,128)S(1)} collective-permute-done((f32[32,2048]{1,0:T(8,128)S(1)}, f32[32,2048]{1,0:T(8,128)S(1)}, u32[]{:S(2)}, u32[]{:S(2)}) %collective-permute-start.7) | collective-permute-done | bytes 262176 | tf_op jit(solution)/shard_map/ppermute | solution.py:128
  41.3 1.2 collective-permute-start.12
  42.6 1.2 collective-permute-start.13
  44.0 1.4 collective-permute-start.24
  45.6 6.6 %shard_map.68 = (f32[7168,896]{1,0:T(8,128)}, f32[512,896]{1,0:T(8,128)S(1)}) custom-call(f32[32,768]{1,0:T(8,128)S(1)} %pad_maximum_fusion.1.refs_0_, f32[32,768]{1,0:T(8,128)S(1)} %slice.136.refs_1_, f32[32,768]{1,0:T(8,128)S(1)} %slice.137.refs_2_, f32[16,768]{1,0:T(8,128)S(1)} %slice.138.refs_3_, f32[16,768]{1,0:T(8,128)S(1)} %slice.139.refs_4_, ...), custom_call_target="tpu_custom_call" | custom-call | flops 4227858432 | bytes 5505024 | tf_op jit(solution)/shard_map/pallas_call | solution.py:67
  52.2 13.4 %collective-permute-done.12.refs_1_ = f32[128,2048]{1,0:T(8,128)S(1)} collective-permute-done((f32[128,2048]{1,0:T(8,128)S(1)}, f32[128,2048]{1,0:T(8,128)S(1)}, u32[]{:S(2)}, u32[]{:S(2)}) %collective-permute-start.12) | collective-permute-done | bytes 1048608 | tf_op jit(solution)/shard_map/ppermute | solution.py:109
  66.9 1.3 collective-permute-start.18
  68.3 1.2 collective-permute-start.25
  69.8 8.6 %collective-permute-done.17.refs_3_ = f32[64,2048]{1,0:T(8,128)S(1)} collective-permute-done((f32[64,2048]{1,0:T(8,128)S(1)}, f32[64,2048]{1,0:T(8,128)S(1)}, u32[]{:S(2)}, u32[]{:S(2)}) %collective-permute-start.17) | collective-permute-done | bytes 524320 | tf_op jit(solution)/shard_map/ppermute | solution.py:109
  78.8 1.1 collective-permute-start.21
  80.0 10.2 %shard_map.69 = (f32[7168,896]{1,0:T(8,128)}, f32[512,896]{1,0:T(8,128)S(1)}) custom-call(f32[128,2048]{1,0:T(8,128)S(1)} %constant_dynamic-update-slice_fusion.refs_0_, f32[128,2048]{1,0:T(8,128)S(1)} %collective-permute-done.12.refs_1_, f32[128,2048]{1,0:T(8,128)S(1)} %collective-permute-done.13.refs_2_, ...), custom_call_target="tpu_custom_call", output_to_operand_aliasing={{1}: (8, {}), {0}: (9, {})} | custom-call | flops 8455716864 | bytes 11010048 | tf_op jit(solution)/shard_map/pallas_call | solution.py:67
  90.3 1.2 collective-permute-start.33
  91.5 2.0 %collective-permute-done.19 = f32[32,1536]{1,0:T(8,128)S(1)} collective-permute-done((f32[32,1536]{1,0:T(8,128)S(1)}, f32[32,1536]{1,0:T(8,128)S(1)}, u32[]{:S(2)}, u32[]{:S(2)}) %collective-permute-start.19) | collective-permute-done | bytes 196640 | tf_op jit(solution)/shard_map/ppermute | solution.py:128
  93.5 1.3 collective-permute-done.21
  94.8 6.0 %collective-permute-done.25.refs_1_ = f32[128,2048]{1,0:T(8,128)S(1)} collective-permute-done((f32[128,2048]{1,0:T(8,128)S(1)}, f32[128,2048]{1,0:T(8,128)S(1)}, u32[]{:S(2)}, u32[]{:S(2)}) %collective-permute-start.25) | collective-permute-done | bytes 1048608 | tf_op jit(solution)/shard_map/ppermute | solution.py:109
  101.0 1.2 collective-permute-start.29
  102.2 1.3 collective-permute-start.30
  103.9 10.2 %shard_map.70 = (f32[7168,896]{1,0:T(8,128)}, f32[512,896]{1,0:T(8,128)S(1)}) custom-call(f32[128,2048]{1,0:T(8,128)S(1)} %constant_dynamic-update-slice_fusion.refs_0_, f32[128,2048]{1,0:T(8,128)S(1)} %collective-permute-done.12.refs_1_, f32[128,2048]{1,0:T(8,128)S(1)} %collective-permute-done.13.refs_2_, ...), custom_call_target="tpu_custom_call", output_to_operand_aliasing={{1}: (8, {}), {0}: (9, {})} | custom-call | flops 8455716864 | bytes 11010048 | tf_op jit(solution)/shard_map/pallas_call | solution.py:67
  114.2 1.7 collective-permute-done.33.refs_1_
  115.8 1.2 collective-permute-start.28
  117.1 2.3 %collective-permute-start.34 = (f32[128,1024]{1,0:T(8,128)S(1)}, f32[128,1024]{1,0:T(8,128)S(1)}, u32[]{:S(2)}, u32[]{:S(2)}) collective-permute-start(f32[128,1024]{1,0:T(8,128)S(1)} %collective-permute-done.33.refs_1_), channel_id=1, source_target_pairs={{0,4},{1,5},{2,6},{3,7},{4,8},{5,9},{6,10},{7,11},{8,12},{9,13},{1... | collective-permute-start | bytes 1572872 | tf_op jit(solution)/shard_map/ppermute | solution.py:109
  119.4 10.2 %shard_map.71 = (f32[7168,896]{1,0:T(8,128)}, f32[512,896]{1,0:T(8,128)S(1)}) custom-call(f32[128,2048]{1,0:T(8,128)S(1)} %constant_dynamic-update-slice_fusion.18.refs_0_, f32[128,2048]{1,0:T(8,128)S(1)} %collective-permute-done.25.refs_1_, f32[128,2048]{1,0:T(8,128)S(1)} %collective-permute-done.26.refs_2_, ...), custom_call_target="tpu_custom_call", output_to_operand_aliasing={{1}: (8, {}), {0}: (9, {})} | custom-call | flops 8455716864 | bytes 11010048 | tf_op jit(solution)/shard_map/pallas_call | solution.py:67
  129.7 2.2 %collective-permute-done.28.refs_2_ = f32[128,1536]{1,0:T(8,128)S(1)} collective-permute-done((f32[128,1536]{1,0:T(8,128)S(1)}, f32[128,1536]{1,0:T(8,128)S(1)}, u32[]{:S(2)}, u32[]{:S(2)}) %collective-permute-start.28) | collective-permute-done | bytes 786464 | tf_op jit(solution)/shard_map/ppermute | solution.py:109
  131.9 1.2 collective-permute-start.31
  133.1 1.3 collective-permute-start.32
  134.4 10.2 %shard_map.72 = (f32[7168,896]{1,0:T(8,128)}, f32[512,896]{1,0:T(8,128)S(1)}) custom-call(f32[128,2048]{1,0:T(8,128)S(1)} %constant_dynamic-update-slice_fusion.18.refs_0_, f32[128,2048]{1,0:T(8,128)S(1)} %collective-permute-done.25.refs_1_, f32[128,2048]{1,0:T(8,128)S(1)} %collective-permute-done.26.refs_2_, ...), custom_call_target="tpu_custom_call", output_to_operand_aliasing={{1}: (8, {}), {0}: (9, {})} | custom-call | flops 8455716864 | bytes 11010048 | tf_op jit(solution)/shard_map/pallas_call | solution.py:67
  144.7 10.2 %shard_map.73 = (f32[7168,896]{1,0:T(8,128)}, f32[512,896]{1,0:T(8,128)S(1)}) custom-call(f32[128,1024]{1,0:T(8,128)S(1)} %slice_dynamic-update-slice_fusion.5.refs_0_, f32[128,1024]{1,0:T(8,128)S(1)} %collective-permute-done.33.refs_1_, f32[128,1024]{1,0:T(8,128)S(1)} %collective-permute-done.34.refs_2_, ...), custom_call_target="tpu_custom_call", output_to_operand_aliasing={{1}: (7, {}), {0}: (8, {})} | custom-call | flops 8455716864 | bytes 11010048 | tf_op jit(solution)/shard_map/pallas_call | solution.py:67
  154.9 14.2 %shard_map.74 = (f32[7168,896]{1,0:T(8,128)}, f32[512,896]{1,0:T(8,128)S(1)}) custom-call(f32[128,1536]{1,0:T(8,128)S(1)} %constant_dynamic-update-slice_fusion.14.refs_0_, f32[128,1536]{1,0:T(8,128)S(1)} %collective-permute-done.27.refs_1_, f32[128,1536]{1,0:T(8,128)S(1)} %collective-permute-done.28.refs_2_, ...), custom_call_target="tpu_custom_call", output_to_operand_aliasing={{1}: (8, {}), {0}: (9, {})} | custom-call | flops 12683575296 | bytes 16515072 | tf_op jit(solution)/shard_map/pallas_call | solution.py:67
  169.1 4.6 %collective-permute-start.36 = (f32[512,896]{1,0:T(8,128)S(1)}, f32[512,896]{1,0:T(8,128)S(1)}, u32[]{:S(2)}, u32[]{:S(2)}) collective-permute-start(f32[512,896]{1,0:T(8,128)S(1)} %get-tuple-element.65), channel_id=1, source_target_pairs={{0,16},{16,0},{1,17},{17,1},{2,18},{18,2},{3,19},{19,3},{4,20},{20... | collective-permute-start | bytes 5505032 | tf_op jit(solution)/shard_map/ppermute | solution.py:113
  173.7 3.4 %collective-permute-done.36 = f32[512,896]{1,0:T(8,128)S(1)} collective-permute-done((f32[512,896]{1,0:T(8,128)S(1)}, f32[512,896]{1,0:T(8,128)S(1)}, u32[]{:S(2)}, u32[]{:S(2)}) %collective-permute-start.36) | collective-permute-done | bytes 1835040 | tf_op jit(solution)/shard_map/ppermute | solution.py:113
  177.1 2.0 %fusion = f32[256,896]{1,0:T(8,128)} fusion(f32[512,256]{1,0:T(8,128)S(1)} %copy-done.3, f32[512,896]{1,0:T(8,128)S(1)} %get-tuple-element.65, f32[512,896]{1,0:T(8,128)S(1)} %collective-permute-done.36), kind=kOutput, calls=%fused_computation | convolution fusion | flops 705101824 | bytes 5111808 | tf_op jit(solution)/shard_map/dot_general | solution.py:196
  (93 shorter events, 7.9 us)
Async XLA Ops:
  0.6 31.0 %copy-start = (f32[256,896]{1,0:T(8,128)S(1)}, f32[256,896]{1,0:T(8,128)}, u32[]{:S(2)}) copy-start(f32[256,896]{1,0:T(8,128)} %param.7) | copy-start | bytes 2752516
  2.4 8.3 %collective-permute-start.2 = (f32[32,768]{1,0:T(8,128)S(1)}, f32[32,768]{1,0:T(8,128)S(1)}, u32[]{:S(2)}, u32[]{:S(2)}) collective-permute-start(f32[32,768]{1,0:T(8,128)S(1)} %pad_maximum_fusion.1.refs_0_), channel_id=1, source_target_pairs={{0,4},{1,5},{2,6},{3,7},{4,8},{5,9},{6,10},{7,11},{8,12},{9,13},{1... | collective-permute-start | bytes 294920 | tf_op jit(solution)/shard_map/ppermute | solution.py:128
  3.7 7.9 %collective-permute-start.3 = (f32[32,768]{1,0:T(8,128)S(1)}, f32[32,768]{1,0:T(8,128)S(1)}, u32[]{:S(2)}, u32[]{:S(2)}) collective-permute-start(f32[32,768]{1,0:T(8,128)S(1)} %pad_maximum_fusion.1.refs_0_), channel_id=1, source_target_pairs={{0,8},{1,9},{2,10},{3,11},{4,12},{5,13},{6,14},{7,15},{8,0},{9,1},... | collective-permute-start | bytes 294920 | tf_op jit(solution)/shard_map/ppermute | solution.py:128
  4.8 9.5 %collective-permute-start.4 = (f32[32,768]{1,0:T(8,128)S(1)}, f32[32,768]{1,0:T(8,128)S(1)}, u32[]{:S(2)}, u32[]{:S(2)}) collective-permute-start(f32[32,768]{1,0:T(8,128)S(1)} %pad_maximum_fusion.1.refs_0_), channel_id=1, source_target_pairs={{0,12},{1,13},{2,14},{3,15},{4,0},{5,1},{6,2},{7,3},{8,4},{9,5},{1... | collective-permute-start | bytes 294920 | tf_op jit(solution)/shard_map/ppermute | solution.py:128
  7.1 7.2 %collective-permute-start = (f32[32,1792]{1,0:T(8,128)S(1)}, f32[32,1792]{1,0:T(8,128)S(1)}, u32[]{:S(2)}, u32[]{:S(2)}) collective-permute-start(f32[32,1792]{1,0:T(8,128)S(1)} %pad_maximum_fusion), channel_id=1, source_target_pairs={{0,1},{1,0},{2,3},{3,2},{4,5},{5,4},{6,7},{7,6},{8,9},{9,8},{10,11... | collective-permute-start | bytes 688136 | tf_op jit(solution)/shard_map/ppermute | solution.py:109
  8.4 6.0 %collective-permute-start.1 = (f32[32,1792]{1,0:T(8,128)S(1)}, f32[32,1792]{1,0:T(8,128)S(1)}, u32[]{:S(2)}, u32[]{:S(2)}) collective-permute-start(f32[32,1792]{1,0:T(8,128)S(1)} %pad_maximum_fusion), channel_id=1, source_target_pairs={{0,2},{1,3},{2,0},{3,1},{4,6},{5,7},{6,4},{7,5},{8,10},{9,11},{10,... | collective-permute-start | bytes 688136 | tf_op jit(solution)/shard_map/ppermute | solution.py:109
  14.4 3.7 %collective-permute-start.8 = (f32[16,1792]{1,0:T(8,128)S(1)}, f32[16,1792]{1,0:T(8,128)S(1)}, u32[]{:S(2)}, u32[]{:S(2)}) collective-permute-start(f32[16,1792]{1,0:T(8,128)S(1)} %slice.104), channel_id=1, source_target_pairs={{0,1},{1,0},{2,3},{3,2},{4,5},{5,4},{6,7},{7,6},{8,9},{9,8},{10,11... | collective-permute-start | bytes 344072 | tf_op jit(solution)/shard_map/ppermute | solution.py:109
  15.7 4.0 %collective-permute-start.9 = (f32[16,1792]{1,0:T(8,128)S(1)}, f32[16,1792]{1,0:T(8,128)S(1)}, u32[]{:S(2)}, u32[]{:S(2)}) collective-permute-start(f32[16,1792]{1,0:T(8,128)S(1)} %slice.105), channel_id=1, source_target_pairs={{0,2},{1,3},{2,0},{3,1},{4,6},{5,7},{6,4},{7,5},{8,10},{9,11},{10,... | collective-permute-start | bytes 344072 | tf_op jit(solution)/shard_map/ppermute | solution.py:109
  16.0 21.4 %collective-permute-start.5 = (f32[32,2048]{1,0:T(8,128)S(1)}, f32[32,2048]{1,0:T(8,128)S(1)}, u32[]{:S(2)}, u32[]{:S(2)}) collective-permute-start(f32[32,2048]{1,0:T(8,128)S(1)} %get-tuple-element.34), channel_id=1, source_target_pairs={{0,4},{1,5},{2,6},{3,7},{4,8},{5,9},{6,10},{7,11},{8,12},{9,13},{1... | collective-permute-start | bytes 786440 | tf_op jit(solution)/shard_map/ppermute | solution.py:128
  16.0 21.3 %collective-permute-start.6 = (f32[32,2048]{1,0:T(8,128)S(1)}, f32[32,2048]{1,0:T(8,128)S(1)}, u32[]{:S(2)}, u32[]{:S(2)}) collective-permute-start(f32[32,2048]{1,0:T(8,128)S(1)} %get-tuple-element.34), channel_id=1, source_target_pairs={{0,8},{1,9},{2,10},{3,11},{4,12},{5,13},{6,14},{7,15},{8,0},{9,1},... | collective-permute-start | bytes 786440 | tf_op jit(solution)/shard_map/ppermute | solution.py:128
  17.6 23.7 %collective-permute-start.7 = (f32[32,2048]{1,0:T(8,128)S(1)}, f32[32,2048]{1,0:T(8,128)S(1)}, u32[]{:S(2)}, u32[]{:S(2)}) collective-permute-start(f32[32,2048]{1,0:T(8,128)S(1)} %get-tuple-element.34), channel_id=1, source_target_pairs={{0,12},{1,13},{2,14},{3,15},{4,0},{5,1},{6,2},{7,3},{8,4},{9,5},{1... | collective-permute-start | bytes 786440 | tf_op jit(solution)/shard_map/ppermute | solution.py:128
  19.7 6.3 %collective-permute-start.10 = (f32[96,768]{1,0:T(8,128)S(1)}, f32[96,768]{1,0:T(8,128)S(1)}, u32[]{:S(2)}, u32[]{:S(2)}) collective-permute-start(f32[96,768]{1,0:T(8,128)S(1)} %constant_dynamic-update-slice_fusion.4.refs_5_), channel_id=1, source_target_pairs={{0,1},{1,0},{2,3},{3,2},{4,5},{5,4},{6,7},{7,6},{8,9},{9,8},{10,11... | collective-permute-start | bytes 884744 | tf_op jit(solution)/shard_map/ppermute | solution.py:109
  19.9 6.0 %collective-permute-start.11 = (f32[96,768]{1,0:T(8,128)S(1)}, f32[96,768]{1,0:T(8,128)S(1)}, u32[]{:S(2)}, u32[]{:S(2)}) collective-permute-start(f32[96,768]{1,0:T(8,128)S(1)} %constant_dynamic-update-slice_fusion.4.refs_5_), channel_id=1, source_target_pairs={{0,2},{1,3},{2,0},{3,1},{4,6},{5,7},{6,4},{7,5},{8,10},{9,11},{10,... | collective-permute-start | bytes 884744 | tf_op jit(solution)/shard_map/ppermute | solution.py:109
  26.0 4.4 %collective-permute-start.14 = (f32[48,768]{1,0:T(8,128)S(1)}, f32[48,768]{1,0:T(8,128)S(1)}, u32[]{:S(2)}, u32[]{:S(2)}) collective-permute-start(f32[48,768]{1,0:T(8,128)S(1)} %slice.110), channel_id=1, source_target_pairs={{0,1},{1,0},{2,3},{3,2},{4,5},{5,4},{6,7},{7,6},{8,9},{9,8},{10,11... | collective-permute-start | bytes 442376 | tf_op jit(solution)/shard_map/ppermute | solution.py:109
  27.2 4.4 %collective-permute-start.15 = (f32[48,768]{1,0:T(8,128)S(1)}, f32[48,768]{1,0:T(8,128)S(1)}, u32[]{:S(2)}, u32[]{:S(2)}) collective-permute-start(f32[48,768]{1,0:T(8,128)S(1)} %slice.111), channel_id=1, source_target_pairs={{0,2},{1,3},{2,0},{3,1},{4,6},{5,7},{6,4},{7,5},{8,10},{9,11},{10,... | collective-permute-start | bytes 442376 | tf_op jit(solution)/shard_map/ppermute | solution.py:109
  31.6 5.7 %copy-start.2 = (f32[512,256]{1,0:T(8,128)}, f32[512,256]{1,0:T(8,128)S(1)}, u32[]{:S(2)}) copy-start(f32[512,256]{1,0:T(8,128)S(1)} %constant_dynamic-update-slice_fusion.7) | copy-start | bytes 1572868
  32.6 11.4 %collective-permute-start.16 = (f32[512,896]{1,0:T(8,128)S(1)}, f32[512,896]{1,0:T(8,128)S(1)}, u32[]{:S(2)}, u32[]{:S(2)}) collective-permute-start(f32[512,896]{1,0:T(8,128)S(1)} %fusion.3), channel_id=1, source_target_pairs={{0,16},{16,0},{1,17},{17,1},{2,18},{18,2},{3,19},{19,3},{4,20},{20... | collective-permute-start | bytes 5505032 | tf_op jit(solution)/shard_map/ppermute | solution.py:113
  41.3 24.3 %collective-permute-start.12 = (f32[128,2048]{1,0:T(8,128)S(1)}, f32[128,2048]{1,0:T(8,128)S(1)}, u32[]{:S(2)}, u32[]{:S(2)}) collective-permute-start(f32[128,2048]{1,0:T(8,128)S(1)} %constant_dynamic-update-slice_fusion.refs_0_), channel_id=1, source_target_pairs={{0,1},{1,0},{2,3},{3,2},{4,5},{5,4},{6,7},{7,6},{8,9},{9,8},{10,11... | collective-permute-start | bytes 3145736 | tf_op jit(solution)/shard_map/ppermute | solution.py:109
  42.6 23.9 %collective-permute-start.13 = (f32[128,2048]{1,0:T(8,128)S(1)}, f32[128,2048]{1,0:T(8,128)S(1)}, u32[]{:S(2)}, u32[]{:S(2)}) collective-permute-start(f32[128,2048]{1,0:T(8,128)S(1)} %constant_dynamic-update-slice_fusion.refs_0_), channel_id=1, source_target_pairs={{0,2},{1,3},{2,0},{3,1},{4,6},{5,7},{6,4},{7,5},{8,10},{9,11},{10,... | collective-permute-start | bytes 3145736 | tf_op jit(solution)/shard_map/ppermute | solution.py:109
  43.8 24.4 %collective-permute-start.22 = (f32[32,2048]{1,0:T(8,128)S(1)}, f32[32,2048]{1,0:T(8,128)S(1)}, u32[]{:S(2)}, u32[]{:S(2)}) collective-permute-start(f32[32,2048]{1,0:T(8,128)S(1)} %get-tuple-element.45), channel_id=1, source_target_pairs={{0,4},{1,5},{2,6},{3,7},{4,8},{5,9},{6,10},{7,11},{8,12},{9,13},{1... | collective-permute-start | bytes 786440 | tf_op jit(solution)/shard_map/ppermute | solution.py:128
  43.9 24.4 %collective-permute-start.23 = (f32[32,2048]{1,0:T(8,128)S(1)}, f32[32,2048]{1,0:T(8,128)S(1)}, u32[]{:S(2)}, u32[]{:S(2)}) collective-permute-start(f32[32,2048]{1,0:T(8,128)S(1)} %get-tuple-element.45), channel_id=1, source_target_pairs={{0,8},{1,9},{2,10},{3,11},{4,12},{5,13},{6,14},{7,15},{8,0},{9,1},... | collective-permute-start | bytes 786440 | tf_op jit(solution)/shard_map/ppermute | solution.py:128
  44.0 24.3 %collective-permute-start.24 = (f32[32,2048]{1,0:T(8,128)S(1)}, f32[32,2048]{1,0:T(8,128)S(1)}, u32[]{:S(2)}, u32[]{:S(2)}) collective-permute-start(f32[32,2048]{1,0:T(8,128)S(1)} %get-tuple-element.45), channel_id=1, source_target_pairs={{0,12},{1,13},{2,14},{3,15},{4,0},{5,1},{6,2},{7,3},{8,4},{9,5},{1... | collective-permute-start | bytes 786440 | tf_op jit(solution)/shard_map/ppermute | solution.py:128
  66.5 11.8 %collective-permute-start.17 = (f32[64,2048]{1,0:T(8,128)S(1)}, f32[64,2048]{1,0:T(8,128)S(1)}, u32[]{:S(2)}, u32[]{:S(2)}) collective-permute-start(f32[64,2048]{1,0:T(8,128)S(1)} %slice.121), channel_id=1, source_target_pairs={{0,1},{1,0},{2,3},{3,2},{4,5},{5,4},{6,7},{7,6},{8,9},{9,8},{10,11... | collective-permute-start | bytes 1572872 | tf_op jit(solution)/shard_map/ppermute | solution.py:109
  66.9 11.6 %collective-permute-start.18 = (f32[64,2048]{1,0:T(8,128)S(1)}, f32[64,2048]{1,0:T(8,128)S(1)}, u32[]{:S(2)}, u32[]{:S(2)}) collective-permute-start(f32[64,2048]{1,0:T(8,128)S(1)} %slice.122), channel_id=1, source_target_pairs={{0,2},{1,3},{2,0},{3,1},{4,6},{5,7},{6,4},{7,5},{8,10},{9,11},{10,... | collective-permute-start | bytes 1572872 | tf_op jit(solution)/shard_map/ppermute | solution.py:109
  68.3 32.5 %collective-permute-start.25 = (f32[128,2048]{1,0:T(8,128)S(1)}, f32[128,2048]{1,0:T(8,128)S(1)}, u32[]{:S(2)}, u32[]{:S(2)}) collective-permute-start(f32[128,2048]{1,0:T(8,128)S(1)} %constant_dynamic-update-slice_fusion.18.refs_0_), channel_id=1, source_target_pairs={{0,1},{1,0},{2,3},{3,2},{4,5},{5,4},{6,7},{7,6},{8,9},{9,8},{10,11... | collective-permute-start | bytes 3145736 | tf_op jit(solution)/shard_map/ppermute | solution.py:109
  69.5 31.4 %collective-permute-start.26 = (f32[128,2048]{1,0:T(8,128)S(1)}, f32[128,2048]{1,0:T(8,128)S(1)}, u32[]{:S(2)}, u32[]{:S(2)}) collective-permute-start(f32[128,2048]{1,0:T(8,128)S(1)} %constant_dynamic-update-slice_fusion.18.refs_0_), channel_id=1, source_target_pairs={{0,2},{1,3},{2,0},{3,1},{4,6},{5,7},{6,4},{7,5},{8,10},{9,11},{10,... | collective-permute-start | bytes 3145736 | tf_op jit(solution)/shard_map/ppermute | solution.py:109
  78.5 11.7 %collective-permute-start.20 = (f32[32,1536]{1,0:T(8,128)S(1)}, f32[32,1536]{1,0:T(8,128)S(1)}, u32[]{:S(2)}, u32[]{:S(2)}) collective-permute-start(f32[32,1536]{1,0:T(8,128)S(1)} %slice.132), channel_id=1, source_target_pairs={{0,8},{1,9},{2,10},{3,11},{4,12},{5,13},{6,14},{7,15},{8,0},{9,1},... | collective-permute-start | bytes 589832 | tf_op jit(solution)/shard_map/ppermute | solution.py:128
  78.5 15.0 %collective-permute-start.19 = (f32[32,1536]{1,0:T(8,128)S(1)}, f32[32,1536]{1,0:T(8,128)S(1)}, u32[]{:S(2)}, u32[]{:S(2)}) collective-permute-start(f32[32,1536]{1,0:T(8,128)S(1)} %slice.132), channel_id=1, source_target_pairs={{0,4},{1,5},{2,6},{3,7},{4,8},{5,9},{6,10},{7,11},{8,12},{9,13},{1... | collective-permute-start | bytes 589832 | tf_op jit(solution)/shard_map/ppermute | solution.py:128
  78.8 15.9 %collective-permute-start.21 = (f32[32,1536]{1,0:T(8,128)S(1)}, f32[32,1536]{1,0:T(8,128)S(1)}, u32[]{:S(2)}, u32[]{:S(2)}) collective-permute-start(f32[32,1536]{1,0:T(8,128)S(1)} %slice.132), channel_id=1, source_target_pairs={{0,12},{1,13},{2,14},{3,15},{4,0},{5,1},{6,2},{7,3},{8,4},{9,5},{1... | collective-permute-start | bytes 589832 | tf_op jit(solution)/shard_map/ppermute | solution.py:128
  90.3 25.6 %collective-permute-start.33 = (f32[128,1024]{1,0:T(8,128)S(1)}, f32[128,1024]{1,0:T(8,128)S(1)}, u32[]{:S(2)}, u32[]{:S(2)}) collective-permute-start(f32[128,1024]{1,0:T(8,128)S(1)} %slice_dynamic-update-slice_fusion.5.refs_0_), channel_id=1, source_target_pairs={{0,4},{1,5},{2,6},{3,7},{4,8},{5,9},{6,10},{7,11},{8,12},{9,13},{1... | collective-permute-start | bytes 1572872 | tf_op jit(solution)/shard_map/ppermute | solution.py:109
  93.5 51.2 %collective-permute-start.35 = (f32[128,1024]{1,0:T(8,128)S(1)}, f32[128,1024]{1,0:T(8,128)S(1)}, u32[]{:S(2)}, u32[]{:S(2)}) collective-permute-start(f32[128,1024]{1,0:T(8,128)S(1)} %slice_dynamic-update-slice_fusion.5.refs_0_), channel_id=1, source_target_pairs={{0,12},{1,13},{2,14},{3,15},{4,0},{5,1},{6,2},{7,3},{8,4},{9,5},{1... | collective-permute-start | bytes 1572872 | tf_op jit(solution)/shard_map/ppermute | solution.py:109
  101.0 16.0 %collective-permute-start.29 = (f32[64,2048]{1,0:T(8,128)S(1)}, f32[64,2048]{1,0:T(8,128)S(1)}, u32[]{:S(2)}, u32[]{:S(2)}) collective-permute-start(f32[64,2048]{1,0:T(8,128)S(1)} %slice.124), channel_id=1, source_target_pairs={{0,1},{1,0},{2,3},{3,2},{4,5},{5,4},{6,7},{7,6},{8,9},{9,8},{10,11... | collective-permute-start | bytes 1572872 | tf_op jit(solution)/shard_map/ppermute | solution.py:109
  102.2 17.2 %collective-permute-start.30 = (f32[64,2048]{1,0:T(8,128)S(1)}, f32[64,2048]{1,0:T(8,128)S(1)}, u32[]{:S(2)}, u32[]{:S(2)}) collective-permute-start(f32[64,2048]{1,0:T(8,128)S(1)} %slice.125), channel_id=1, source_target_pairs={{0,2},{1,3},{2,0},{3,1},{4,6},{5,7},{6,4},{7,5},{8,10},{9,11},{10,... | collective-permute-start | bytes 1572872 | tf_op jit(solution)/shard_map/ppermute | solution.py:109
  103.5 26.1 %collective-permute-start.27 = (f32[128,1536]{1,0:T(8,128)S(1)}, f32[128,1536]{1,0:T(8,128)S(1)}, u32[]{:S(2)}, u32[]{:S(2)}) collective-permute-start(f32[128,1536]{1,0:T(8,128)S(1)} %constant_dynamic-update-slice_fusion.14.refs_0_), channel_id=1, source_target_pairs={{0,1},{1,0},{2,3},{3,2},{4,5},{5,4},{6,7},{7,6},{8,9},{9,8},{10,11... | collective-permute-start | bytes 2359304 | tf_op jit(solution)/shard_map/ppermute | solution.py:109
  115.8 16.1 %collective-permute-start.28 = (f32[128,1536]{1,0:T(8,128)S(1)}, f32[128,1536]{1,0:T(8,128)S(1)}, u32[]{:S(2)}, u32[]{:S(2)}) collective-permute-start(f32[128,1536]{1,0:T(8,128)S(1)} %constant_dynamic-update-slice_fusion.14.refs_0_), channel_id=1, source_target_pairs={{0,2},{1,3},{2,0},{3,1},{4,6},{5,7},{6,4},{7,5},{8,10},{9,11},{10,... | collective-permute-start | bytes 2359304 | tf_op jit(solution)/shard_map/ppermute | solution.py:109
  117.1 27.6 %collective-permute-start.34 = (f32[128,1024]{1,0:T(8,128)S(1)}, f32[128,1024]{1,0:T(8,128)S(1)}, u32[]{:S(2)}, u32[]{:S(2)}) collective-permute-start(f32[128,1024]{1,0:T(8,128)S(1)} %collective-permute-done.33.refs_1_), channel_id=1, source_target_pairs={{0,4},{1,5},{2,6},{3,7},{4,8},{5,9},{6,10},{7,11},{8,12},{9,13},{1... | collective-permute-start | bytes 1572872 | tf_op jit(solution)/shard_map/ppermute | solution.py:109
  131.9 23.0 %collective-permute-start.31 = (f32[64,1536]{1,0:T(8,128)S(1)}, f32[64,1536]{1,0:T(8,128)S(1)}, u32[]{:S(2)}, u32[]{:S(2)}) collective-permute-start(f32[64,1536]{1,0:T(8,128)S(1)} %slice.126), channel_id=1, source_target_pairs={{0,1},{1,0},{2,3},{3,2},{4,5},{5,4},{6,7},{7,6},{8,9},{9,8},{10,11... | collective-permute-start | bytes 1179656 | tf_op jit(solution)/shard_map/ppermute | solution.py:109
  133.1 21.8 %collective-permute-start.32 = (f32[64,1536]{1,0:T(8,128)S(1)}, f32[64,1536]{1,0:T(8,128)S(1)}, u32[]{:S(2)}, u32[]{:S(2)}) collective-permute-start(f32[64,1536]{1,0:T(8,128)S(1)} %slice.127), channel_id=1, source_target_pairs={{0,2},{1,3},{2,0},{3,1},{4,6},{5,7},{6,4},{7,5},{8,10},{9,11},{10,... | collective-permute-start | bytes 1179656 | tf_op jit(solution)/shard_map/ppermute | solution.py:109
  154.9 22.2 %copy-start.3 = (f32[512,256]{1,0:T(8,128)S(1)}, f32[512,256]{1,0:T(8,128)}, u32[]{:S(2)}) copy-start(f32[512,256]{1,0:T(8,128)} %copy-done.2) | copy-start | bytes 1572868
  169.1 10.0 %copy-start.1 = (f32[256,896]{1,0:T(8,128)S(1)}, f32[256,896]{1,0:T(8,128)}, u32[]{:S(2)}) copy-start(f32[256,896]{1,0:T(8,128)} %param.7) | copy-start | bytes 2752516
  169.1 8.0 %collective-permute-start.36 = (f32[512,896]{1,0:T(8,128)S(1)}, f32[512,896]{1,0:T(8,128)S(1)}, u32[]{:S(2)}, u32[]{:S(2)}) collective-permute-start(f32[512,896]{1,0:T(8,128)S(1)} %get-tuple-element.65), channel_id=1, source_target_pairs={{0,16},{16,0},{1,17},{17,1},{2,18},{18,2},{3,19},{19,3},{4,20},{20... | collective-permute-start | bytes 5505032 | tf_op jit(solution)/shard_map/ppermute | solution.py:113

commit v3 on v2

--- a/solution.py
+++ b/solution.py
@@ -187,7 +187,7 @@
     d4 = jnp.concatenate(z4, 0)
     x4, y4 = cross(d4, x3, y3, s2a[1])
     plane = jnp.concatenate([p[:, wide1:] for p in (early, x0, y0, *xy0)], 0)
-    z5 = near(plane, z4[2], s2a[1])
+    z5 = near(plane, z4[2])
     s3a, s3 = halves([d3, x3, y3, *xy3], s2, 2)
     xy4 = corner(x4, y4, s3a[1])
     z5 = far(plane, *z5)

time: 180 us -> 182 us (1.011)
  starting transfers between devices: 38.4 us -> 42.8 us
  waiting for transfers between devices: 59.3 us -> 55.3 us
    ppermute x2, starting transfers between devices: 9.25 us -> 14.5 us  [over_row(): return x + lax.ppermute(after(x, *done), 'row', [(0, 1), (1, 0)])]
    ppermute x23, waiting for transfers between devices: 45.1 us -> 41.3 us  [send(): return lax.ppermute(after(x, *done), 'col', pairs[way])]
  transfers between devices with their start and end apart: 37 -> 37, of which waited for: 19 -> 18; matrix products, arithmetic and copies ran while one was open for 3% -> 3% of each run, Pallas kernels for 32% -> 32%
where the time goes in v3:
time: 182 us; the launch traced here: 179 us
  Pallas kernels  72 us (40%)
  waiting for transfers between devices  55.3 us (30%)
  starting transfers between devices  42.8 us (24%)
  local copies, waits for them, and re-layouts  5.22 us (3%)
  matrix products  2.97 us (2%)
    pallas_call x7, Pallas kernels, panel_step(): pl.pallas_call(functools.partial(panel_kernel, places, first), grid=(size...  72 us
    ppermute x23, waiting for transfers between devices, send(): return lax.ppermute(after(x, *done), 'col', pairs[way])  41.3 us
    ppermute x23, starting transfers between devices, send(): return lax.ppermute(after(x, *done), 'col', pairs[way])  19.9 us
    ppermute x2, starting transfers between devices, over_row(): return x + lax.ppermute(after(x, *done), 'row', [(0, 1), (1, 0)])  14.5 us
    ppermute x12, waiting for transfers between devices, along_z(): lax.ppermute(block, 'col', [(c, (c + 4 * j) % n_col) for c in range(n_col)])  10.5 us
    ppermute x12, starting transfers between devices, along_z(): lax.ppermute(block, 'col', [(c, (c + 4 * j) % n_col) for c in range(n_col)])  8.45 us
  transfers between devices with their start and end apart: 37, of which 18 were waited for; matrix products, arithmetic and copies ran while one was open for 3% of the time, Pallas kernels for 32%

profile of v3, /device:TPU:13, one launch (start us, length us, event | category | flops | bytes accessed | tf_op | source)
XLA Modules:
  0.0 179.5 jit_solution(10847186320710922124)
XLA Ops:
  0.7 0.9 slice.134
  1.6 0.8 constant_dynamic-update-slice_fusion.13
  2.4 1.3 collective-permute-start.2
  3.7 1.1 collective-permute-start.3
  4.8 1.4 collective-permute-start.4
  6.2 0.9 constant_dynamic-update-slice_fusion.22
  7.1 1.3 collective-permute-start
  8.6 1.1 fusion.2
  9.7 0.9 slice.132
  10.7 0.9 collective-permute-done.3
  11.6 2.7 %collective-permute-done.4 = f32[32,768]{1,0:T(8,128)S(1)} collective-permute-done((f32[32,768]{1,0:T(8,128)S(1)}, f32[32,768]{1,0:T(8,128)S(1)}, u32[]{:S(2)}, u32[]{:S(2)}) %collective-permute-start.4) | collective-permute-done | bytes 98336 | tf_op jit(solution)/shard_map/ppermute | solution.py:128
  14.4 1.3 collective-permute-start.8
  16.0 1.5 collective-permute-start.6
  18.1 1.6 collective-permute-done.9
  20.2 5.8 %collective-permute-done.10.refs_6_ = f32[96,768]{1,0:T(8,128)S(1)} collective-permute-done((f32[96,768]{1,0:T(8,128)S(1)}, f32[96,768]{1,0:T(8,128)S(1)}, u32[]{:S(2)}, u32[]{:S(2)}) %collective-permute-start.10) | collective-permute-done | bytes 294944 | tf_op jit(solution)/shard_map/ppermute | solution.py:109
  26.0 1.2 collective-permute-start.14
  27.5 2.9 %collective-permute-done.14.refs_8_ = f32[48,768]{1,0:T(8,128)S(1)} collective-permute-done((f32[48,768]{1,0:T(8,128)S(1)}, f32[48,768]{1,0:T(8,128)S(1)}, u32[]{:S(2)}, u32[]{:S(2)}) %collective-permute-start.14) | collective-permute-done | bytes 147488 | tf_op jit(solution)/shard_map/ppermute | solution.py:109
  30.3 1.3 collective-permute-done.15.refs_9_
  31.6 1.0 fusion.3
  32.6 4.6 %collective-permute-start.16 = (f32[512,896]{1,0:T(8,128)S(1)}, f32[512,896]{1,0:T(8,128)S(1)}, u32[]{:S(2)}, u32[]{:S(2)}) collective-permute-start(f32[512,896]{1,0:T(8,128)S(1)} %fusion.3), channel_id=1, source_target_pairs={{0,16},{16,0},{1,17},{17,1},{2,18},{18,2},{3,19},{19,3},{4,20},{20... | collective-permute-start | bytes 5505032 | tf_op jit(solution)/shard_map/ppermute | solution.py:113
  37.4 3.9 %collective-permute-done.7 = f32[32,2048]{1,0:T(8,128)S(1)} collective-permute-done((f32[32,2048]{1,0:T(8,128)S(1)}, f32[32,2048]{1,0:T(8,128)S(1)}, u32[]{:S(2)}, u32[]{:S(2)}) %collective-permute-start.7) | collective-permute-done | bytes 262176 | tf_op jit(solution)/shard_map/ppermute | solution.py:128
  41.3 1.2 collective-permute-start.12
  42.6 1.2 collective-permute-start.13
  44.0 1.4 collective-permute-start.24
  45.6 6.6 %shard_map.68 = (f32[7168,896]{1,0:T(8,128)}, f32[512,896]{1,0:T(8,128)S(1)}) custom-call(f32[32,768]{1,0:T(8,128)S(1)} %pad_maximum_fusion.1.refs_0_, f32[32,768]{1,0:T(8,128)S(1)} %slice.136.refs_1_, f32[32,768]{1,0:T(8,128)S(1)} %slice.137.refs_2_, f32[16,768]{1,0:T(8,128)S(1)} %slice.138.refs_3_, f32[16,768]{1,0:T(8,128)S(1)} %slice.139.refs_4_, ...), custom_call_target="tpu_custom_call" | custom-call | flops 4227858432 | bytes 5505024 | tf_op jit(solution)/shard_map/pallas_call | solution.py:67
  52.2 13.4 %collective-permute-done.12.refs_1_ = f32[128,2048]{1,0:T(8,128)S(1)} collective-permute-done((f32[128,2048]{1,0:T(8,128)S(1)}, f32[128,2048]{1,0:T(8,128)S(1)}, u32[]{:S(2)}, u32[]{:S(2)}) %collective-permute-start.12) | collective-permute-done | bytes 1048608 | tf_op jit(solution)/shard_map/ppermute | solution.py:109
  65.6 0.9 collective-permute-done.13.refs_2_
  66.9 1.3 collective-permute-start.18
  68.3 1.2 collective-permute-start.25
  69.8 8.6 %collective-permute-done.17.refs_3_ = f32[64,2048]{1,0:T(8,128)S(1)} collective-permute-done((f32[64,2048]{1,0:T(8,128)S(1)}, f32[64,2048]{1,0:T(8,128)S(1)}, u32[]{:S(2)}, u32[]{:S(2)}) %collective-permute-start.17) | collective-permute-done | bytes 524320 | tf_op jit(solution)/shard_map/ppermute | solution.py:109
  78.5 1.2 collective-permute-start.20
  80.0 10.2 %shard_map.69 = (f32[7168,896]{1,0:T(8,128)}, f32[512,896]{1,0:T(8,128)S(1)}) custom-call(f32[128,2048]{1,0:T(8,128)S(1)} %constant_dynamic-update-slice_fusion.refs_0_, f32[128,2048]{1,0:T(8,128)S(1)} %collective-permute-done.12.refs_1_, f32[128,2048]{1,0:T(8,128)S(1)} %collective-permute-done.13.refs_2_, ...), custom_call_target="tpu_custom_call", output_to_operand_aliasing={{1}: (8, {}), {0}: (9, {})} | custom-call | flops 8455716864 | bytes 11010048 | tf_op jit(solution)/shard_map/pallas_call | solution.py:67
  90.3 1.3 collective-permute-start.33
  91.5 1.6 collective-permute-start.35
  93.2 3.0 %collective-permute-done.21 = f32[32,1536]{1,0:T(8,128)S(1)} collective-permute-done((f32[32,1536]{1,0:T(8,128)S(1)}, f32[32,1536]{1,0:T(8,128)S(1)}, u32[]{:S(2)}, u32[]{:S(2)}) %collective-permute-start.21) | collective-permute-done | bytes 196640 | tf_op jit(solution)/shard_map/ppermute | solution.py:128
  96.2 4.6 %collective-permute-done.25.refs_1_ = f32[128,2048]{1,0:T(8,128)S(1)} collective-permute-done((f32[128,2048]{1,0:T(8,128)S(1)}, f32[128,2048]{1,0:T(8,128)S(1)}, u32[]{:S(2)}, u32[]{:S(2)}) %collective-permute-start.25) | collective-permute-done | bytes 1048608 | tf_op jit(solution)/shard_map/ppermute | solution.py:109
  101.0 1.2 collective-permute-start.29
  102.2 1.3 collective-permute-start.30
  103.9 10.2 %shard_map.70 = (f32[7168,896]{1,0:T(8,128)}, f32[512,896]{1,0:T(8,128)S(1)}) custom-call(f32[128,2048]{1,0:T(8,128)S(1)} %constant_dynamic-update-slice_fusion.refs_0_, f32[128,2048]{1,0:T(8,128)S(1)} %collective-permute-done.12.refs_1_, f32[128,2048]{1,0:T(8,128)S(1)} %collective-permute-done.13.refs_2_, ...), custom_call_target="tpu_custom_call", output_to_operand_aliasing={{1}: (8, {}), {0}: (9, {})} | custom-call | flops 8455716864 | bytes 11010048 | tf_op jit(solution)/shard_map/pallas_call | solution.py:67
  114.4 10.3 %shard_map.71 = (f32[7168,896]{1,0:T(8,128)}, f32[512,896]{1,0:T(8,128)S(1)}) custom-call(f32[128,2048]{1,0:T(8,128)S(1)} %constant_dynamic-update-slice_fusion.18.refs_0_, f32[128,2048]{1,0:T(8,128)S(1)} %collective-permute-done.25.refs_1_, f32[128,2048]{1,0:T(8,128)S(1)} %collective-permute-done.26.refs_2_, ...), custom_call_target="tpu_custom_call", output_to_operand_aliasing={{1}: (8, {}), {0}: (9, {})} | custom-call | flops 8455716864 | bytes 11010048 | tf_op jit(solution)/shard_map/pallas_call | solution.py:67
  126.2 1.5 collective-permute-start.31
  127.8 1.8 %collective-permute-start.32 = (f32[64,1536]{1,0:T(8,128)S(1)}, f32[64,1536]{1,0:T(8,128)S(1)}, u32[]{:S(2)}, u32[]{:S(2)}) collective-permute-start(f32[64,1536]{1,0:T(8,128)S(1)} %slice.127), channel_id=1, source_target_pairs={{0,2},{1,3},{2,0},{3,1},{4,6},{5,7},{6,4},{7,5},{8,10},{9,11},{10,... | collective-permute-start | bytes 1179656 | tf_op jit(solution)/shard_map/ppermute | solution.py:109
  129.6 10.2 %shard_map.72 = (f32[7168,896]{1,0:T(8,128)}, f32[512,896]{1,0:T(8,128)S(1)}) custom-call(f32[128,2048]{1,0:T(8,128)S(1)} %constant_dynamic-update-slice_fusion.18.refs_0_, f32[128,2048]{1,0:T(8,128)S(1)} %collective-permute-done.25.refs_1_, f32[128,2048]{1,0:T(8,128)S(1)} %collective-permute-done.26.refs_2_, ...), custom_call_target="tpu_custom_call", output_to_operand_aliasing={{1}: (8, {}), {0}: (9, {})} | custom-call | flops 8455716864 | bytes 11010048 | tf_op jit(solution)/shard_map/pallas_call | solution.py:67
  139.8 10.2 %shard_map.73 = (f32[7168,896]{1,0:T(8,128)}, f32[512,896]{1,0:T(8,128)S(1)}) custom-call(f32[128,1024]{1,0:T(8,128)S(1)} %slice_dynamic-update-slice_fusion.5.refs_0_, f32[128,1024]{1,0:T(8,128)S(1)} %collective-permute-done.33.refs_1_, f32[128,1024]{1,0:T(8,128)S(1)} %collective-permute-done.34.refs_2_, ...), custom_call_target="tpu_custom_call", output_to_operand_aliasing={{1}: (7, {}), {0}: (8, {})} | custom-call | flops 8455716864 | bytes 11010048 | tf_op jit(solution)/shard_map/pallas_call | solution.py:67
  150.1 14.2 %shard_map.74 = (f32[7168,896]{1,0:T(8,128)}, f32[512,896]{1,0:T(8,128)S(1)}) custom-call(f32[128,1536]{1,0:T(8,128)S(1)} %constant_dynamic-update-slice_fusion.14.refs_0_, f32[128,1536]{1,0:T(8,128)S(1)} %collective-permute-done.27.refs_1_, f32[128,1536]{1,0:T(8,128)S(1)} %collective-permute-done.28.refs_2_, ...), custom_call_target="tpu_custom_call", output_to_operand_aliasing={{1}: (8, {}), {0}: (9, {})} | custom-call | flops 12683575296 | bytes 16515072 | tf_op jit(solution)/shard_map/pallas_call | solution.py:67
  164.3 9.8 %collective-permute-start.36 = (f32[512,896]{1,0:T(8,128)S(1)}, f32[512,896]{1,0:T(8,128)S(1)}, u32[]{:S(2)}, u32[]{:S(2)}) collective-permute-start(f32[512,896]{1,0:T(8,128)S(1)} %get-tuple-element.65), channel_id=1, source_target_pairs={{0,16},{16,0},{1,17},{17,1},{2,18},{18,2},{3,19},{19,3},{4,20},{20... | collective-permute-start | bytes 5505032 | tf_op jit(solution)/shard_map/ppermute | solution.py:113
  174.1 3.4 %collective-permute-done.36 = f32[512,896]{1,0:T(8,128)S(1)} collective-permute-done((f32[512,896]{1,0:T(8,128)S(1)}, f32[512,896]{1,0:T(8,128)S(1)}, u32[]{:S(2)}, u32[]{:S(2)}) %collective-permute-start.36) | collective-permute-done | bytes 1835040 | tf_op jit(solution)/shard_map/ppermute | solution.py:113
  177.5 2.0 %fusion = f32[256,896]{1,0:T(8,128)} fusion(f32[512,256]{1,0:T(8,128)S(1)} %copy-done.3, f32[512,896]{1,0:T(8,128)S(1)} %get-tuple-element.65, f32[512,896]{1,0:T(8,128)S(1)} %collective-permute-done.36), kind=kOutput, calls=%fused_computation | convolution fusion | flops 705101824 | bytes 5111808 | tf_op jit(solution)/shard_map/dot_general | solution.py:196
  (93 shorter events, 6.1 us)
Async XLA Ops:
  0.6 31.0 %copy-start = (f32[256,896]{1,0:T(8,128)S(1)}, f32[256,896]{1,0:T(8,128)}, u32[]{:S(2)}) copy-start(f32[256,896]{1,0:T(8,128)} %param.7) | copy-start | bytes 2752516
  2.4 8.3 %collective-permute-start.2 = (f32[32,768]{1,0:T(8,128)S(1)}, f32[32,768]{1,0:T(8,128)S(1)}, u32[]{:S(2)}, u32[]{:S(2)}) collective-permute-start(f32[32,768]{1,0:T(8,128)S(1)} %pad_maximum_fusion.1.refs_0_), channel_id=1, source_target_pairs={{0,4},{1,5},{2,6},{3,7},{4,8},{5,9},{6,10},{7,11},{8,12},{9,13},{1... | collective-permute-start | bytes 294920 | tf_op jit(solution)/shard_map/ppermute | solution.py:128
  3.7 7.9 %collective-permute-start.3 = (f32[32,768]{1,0:T(8,128)S(1)}, f32[32,768]{1,0:T(8,128)S(1)}, u32[]{:S(2)}, u32[]{:S(2)}) collective-permute-start(f32[32,768]{1,0:T(8,128)S(1)} %pad_maximum_fusion.1.refs_0_), channel_id=1, source_target_pairs={{0,8},{1,9},{2,10},{3,11},{4,12},{5,13},{6,14},{7,15},{8,0},{9,1},... | collective-permute-start | bytes 294920 | tf_op jit(solution)/shard_map/ppermute | solution.py:128
  4.8 9.5 %collective-permute-start.4 = (f32[32,768]{1,0:T(8,128)S(1)}, f32[32,768]{1,0:T(8,128)S(1)}, u32[]{:S(2)}, u32[]{:S(2)}) collective-permute-start(f32[32,768]{1,0:T(8,128)S(1)} %pad_maximum_fusion.1.refs_0_), channel_id=1, source_target_pairs={{0,12},{1,13},{2,14},{3,15},{4,0},{5,1},{6,2},{7,3},{8,4},{9,5},{1... | collective-permute-start | bytes 294920 | tf_op jit(solution)/shard_map/ppermute | solution.py:128
  7.1 7.2 %collective-permute-start = (f32[32,1792]{1,0:T(8,128)S(1)}, f32[32,1792]{1,0:T(8,128)S(1)}, u32[]{:S(2)}, u32[]{:S(2)}) collective-permute-start(f32[32,1792]{1,0:T(8,128)S(1)} %pad_maximum_fusion), channel_id=1, source_target_pairs={{0,1},{1,0},{2,3},{3,2},{4,5},{5,4},{6,7},{7,6},{8,9},{9,8},{10,11... | collective-permute-start | bytes 688136 | tf_op jit(solution)/shard_map/ppermute | solution.py:109
  8.4 6.0 %collective-permute-start.1 = (f32[32,1792]{1,0:T(8,128)S(1)}, f32[32,1792]{1,0:T(8,128)S(1)}, u32[]{:S(2)}, u32[]{:S(2)}) collective-permute-start(f32[32,1792]{1,0:T(8,128)S(1)} %pad_maximum_fusion), channel_id=1, source_target_pairs={{0,2},{1,3},{2,0},{3,1},{4,6},{5,7},{6,4},{7,5},{8,10},{9,11},{10,... | collective-permute-start | bytes 688136 | tf_op jit(solution)/shard_map/ppermute | solution.py:109
  14.4 3.7 %collective-permute-start.8 = (f32[16,1792]{1,0:T(8,128)S(1)}, f32[16,1792]{1,0:T(8,128)S(1)}, u32[]{:S(2)}, u32[]{:S(2)}) collective-permute-start(f32[16,1792]{1,0:T(8,128)S(1)} %slice.104), channel_id=1, source_target_pairs={{0,1},{1,0},{2,3},{3,2},{4,5},{5,4},{6,7},{7,6},{8,9},{9,8},{10,11... | collective-permute-start | bytes 344072 | tf_op jit(solution)/shard_map/ppermute | solution.py:109
  15.7 4.0 %collective-permute-start.9 = (f32[16,1792]{1,0:T(8,128)S(1)}, f32[16,1792]{1,0:T(8,128)S(1)}, u32[]{:S(2)}, u32[]{:S(2)}) collective-permute-start(f32[16,1792]{1,0:T(8,128)S(1)} %slice.105), channel_id=1, source_target_pairs={{0,2},{1,3},{2,0},{3,1},{4,6},{5,7},{6,4},{7,5},{8,10},{9,11},{10,... | collective-permute-start | bytes 344072 | tf_op jit(solution)/shard_map/ppermute | solution.py:109
  16.0 21.4 %collective-permute-start.5 = (f32[32,2048]{1,0:T(8,128)S(1)}, f32[32,2048]{1,0:T(8,128)S(1)}, u32[]{:S(2)}, u32[]{:S(2)}) collective-permute-start(f32[32,2048]{1,0:T(8,128)S(1)} %get-tuple-element.34), channel_id=1, source_target_pairs={{0,4},{1,5},{2,6},{3,7},{4,8},{5,9},{6,10},{7,11},{8,12},{9,13},{1... | collective-permute-start | bytes 786440 | tf_op jit(solution)/shard_map/ppermute | solution.py:128
  16.0 21.3 %collective-permute-start.6 = (f32[32,2048]{1,0:T(8,128)S(1)}, f32[32,2048]{1,0:T(8,128)S(1)}, u32[]{:S(2)}, u32[]{:S(2)}) collective-permute-start(f32[32,2048]{1,0:T(8,128)S(1)} %get-tuple-element.34), channel_id=1, source_target_pairs={{0,8},{1,9},{2,10},{3,11},{4,12},{5,13},{6,14},{7,15},{8,0},{9,1},... | collective-permute-start | bytes 786440 | tf_op jit(solution)/shard_map/ppermute | solution.py:128
  17.6 23.7 %collective-permute-start.7 = (f32[32,2048]{1,0:T(8,128)S(1)}, f32[32,2048]{1,0:T(8,128)S(1)}, u32[]{:S(2)}, u32[]{:S(2)}) collective-permute-start(f32[32,2048]{1,0:T(8,128)S(1)} %get-tuple-element.34), channel_id=1, source_target_pairs={{0,12},{1,13},{2,14},{3,15},{4,0},{5,1},{6,2},{7,3},{8,4},{9,5},{1... | collective-permute-start | bytes 786440 | tf_op jit(solution)/shard_map/ppermute | solution.py:128
  19.7 6.3 %collective-permute-start.10 = (f32[96,768]{1,0:T(8,128)S(1)}, f32[96,768]{1,0:T(8,128)S(1)}, u32[]{:S(2)}, u32[]{:S(2)}) collective-permute-start(f32[96,768]{1,0:T(8,128)S(1)} %constant_dynamic-update-slice_fusion.4.refs_5_), channel_id=1, source_target_pairs={{0,1},{1,0},{2,3},{3,2},{4,5},{5,4},{6,7},{7,6},{8,9},{9,8},{10,11... | collective-permute-start | bytes 884744 | tf_op jit(solution)/shard_map/ppermute | solution.py:109
  19.9 6.0 %collective-permute-start.11 = (f32[96,768]{1,0:T(8,128)S(1)}, f32[96,768]{1,0:T(8,128)S(1)}, u32[]{:S(2)}, u32[]{:S(2)}) collective-permute-start(f32[96,768]{1,0:T(8,128)S(1)} %constant_dynamic-update-slice_fusion.4.refs_5_), channel_id=1, source_target_pairs={{0,2},{1,3},{2,0},{3,1},{4,6},{5,7},{6,4},{7,5},{8,10},{9,11},{10,... | collective-permute-start | bytes 884744 | tf_op jit(solution)/shard_map/ppermute | solution.py:109
  26.0 4.4 %collective-permute-start.14 = (f32[48,768]{1,0:T(8,128)S(1)}, f32[48,768]{1,0:T(8,128)S(1)}, u32[]{:S(2)}, u32[]{:S(2)}) collective-permute-start(f32[48,768]{1,0:T(8,128)S(1)} %slice.110), channel_id=1, source_target_pairs={{0,1},{1,0},{2,3},{3,2},{4,5},{5,4},{6,7},{7,6},{8,9},{9,8},{10,11... | collective-permute-start | bytes 442376 | tf_op jit(solution)/shard_map/ppermute | solution.py:109
  27.2 4.4 %collective-permute-start.15 = (f32[48,768]{1,0:T(8,128)S(1)}, f32[48,768]{1,0:T(8,128)S(1)}, u32[]{:S(2)}, u32[]{:S(2)}) collective-permute-start(f32[48,768]{1,0:T(8,128)S(1)} %slice.111), channel_id=1, source_target_pairs={{0,2},{1,3},{2,0},{3,1},{4,6},{5,7},{6,4},{7,5},{8,10},{9,11},{10,... | collective-permute-start | bytes 442376 | tf_op jit(solution)/shard_map/ppermute | solution.py:109
  31.6 5.7 %copy-start.2 = (f32[512,256]{1,0:T(8,128)}, f32[512,256]{1,0:T(8,128)S(1)}, u32[]{:S(2)}) copy-start(f32[512,256]{1,0:T(8,128)S(1)} %constant_dynamic-update-slice_fusion.7) | copy-start | bytes 1572868
  32.6 11.4 %collective-permute-start.16 = (f32[512,896]{1,0:T(8,128)S(1)}, f32[512,896]{1,0:T(8,128)S(1)}, u32[]{:S(2)}, u32[]{:S(2)}) collective-permute-start(f32[512,896]{1,0:T(8,128)S(1)} %fusion.3), channel_id=1, source_target_pairs={{0,16},{16,0},{1,17},{17,1},{2,18},{18,2},{3,19},{19,3},{4,20},{20... | collective-permute-start | bytes 5505032 | tf_op jit(solution)/shard_map/ppermute | solution.py:113
  41.3 24.3 %collective-permute-start.12 = (f32[128,2048]{1,0:T(8,128)S(1)}, f32[128,2048]{1,0:T(8,128)S(1)}, u32[]{:S(2)}, u32[]{:S(2)}) collective-permute-start(f32[128,2048]{1,0:T(8,128)S(1)} %constant_dynamic-update-slice_fusion.refs_0_), channel_id=1, source_target_pairs={{0,1},{1,0},{2,3},{3,2},{4,5},{5,4},{6,7},{7,6},{8,9},{9,8},{10,11... | collective-permute-start | bytes 3145736 | tf_op jit(solution)/shard_map/ppermute | solution.py:109
  42.6 23.9 %collective-permute-start.13 = (f32[128,2048]{1,0:T(8,128)S(1)}, f32[128,2048]{1,0:T(8,128)S(1)}, u32[]{:S(2)}, u32[]{:S(2)}) collective-permute-start(f32[128,2048]{1,0:T(8,128)S(1)} %constant_dynamic-update-slice_fusion.refs_0_), channel_id=1, source_target_pairs={{0,2},{1,3},{2,0},{3,1},{4,6},{5,7},{6,4},{7,5},{8,10},{9,11},{10,... | collective-permute-start | bytes 3145736 | tf_op jit(solution)/shard_map/ppermute | solution.py:109
  43.8 24.4 %collective-permute-start.22 = (f32[32,2048]{1,0:T(8,128)S(1)}, f32[32,2048]{1,0:T(8,128)S(1)}, u32[]{:S(2)}, u32[]{:S(2)}) collective-permute-start(f32[32,2048]{1,0:T(8,128)S(1)} %get-tuple-element.45), channel_id=1, source_target_pairs={{0,4},{1,5},{2,6},{3,7},{4,8},{5,9},{6,10},{7,11},{8,12},{9,13},{1... | collective-permute-start | bytes 786440 | tf_op jit(solution)/shard_map/ppermute | solution.py:128
  43.9 24.4 %collective-permute-start.23 = (f32[32,2048]{1,0:T(8,128)S(1)}, f32[32,2048]{1,0:T(8,128)S(1)}, u32[]{:S(2)}, u32[]{:S(2)}) collective-permute-start(f32[32,2048]{1,0:T(8,128)S(1)} %get-tuple-element.45), channel_id=1, source_target_pairs={{0,8},{1,9},{2,10},{3,11},{4,12},{5,13},{6,14},{7,15},{8,0},{9,1},... | collective-permute-start | bytes 786440 | tf_op jit(solution)/shard_map/ppermute | solution.py:128
  44.0 24.3 %collective-permute-start.24 = (f32[32,2048]{1,0:T(8,128)S(1)}, f32[32,2048]{1,0:T(8,128)S(1)}, u32[]{:S(2)}, u32[]{:S(2)}) collective-permute-start(f32[32,2048]{1,0:T(8,128)S(1)} %get-tuple-element.45), channel_id=1, source_target_pairs={{0,12},{1,13},{2,14},{3,15},{4,0},{5,1},{6,2},{7,3},{8,4},{9,5},{1... | collective-permute-start | bytes 786440 | tf_op jit(solution)/shard_map/ppermute | solution.py:128
  66.5 11.8 %collective-permute-start.17 = (f32[64,2048]{1,0:T(8,128)S(1)}, f32[64,2048]{1,0:T(8,128)S(1)}, u32[]{:S(2)}, u32[]{:S(2)}) collective-permute-start(f32[64,2048]{1,0:T(8,128)S(1)} %slice.121), channel_id=1, source_target_pairs={{0,1},{1,0},{2,3},{3,2},{4,5},{5,4},{6,7},{7,6},{8,9},{9,8},{10,11... | collective-permute-start | bytes 1572872 | tf_op jit(solution)/shard_map/ppermute | solution.py:109
  66.9 11.6 %collective-permute-start.18 = (f32[64,2048]{1,0:T(8,128)S(1)}, f32[64,2048]{1,0:T(8,128)S(1)}, u32[]{:S(2)}, u32[]{:S(2)}) collective-permute-start(f32[64,2048]{1,0:T(8,128)S(1)} %slice.122), channel_id=1, source_target_pairs={{0,2},{1,3},{2,0},{3,1},{4,6},{5,7},{6,4},{7,5},{8,10},{9,11},{10,... | collective-permute-start | bytes 1572872 | tf_op jit(solution)/shard_map/ppermute | solution.py:109
  68.3 32.5 %collective-permute-start.25 = (f32[128,2048]{1,0:T(8,128)S(1)}, f32[128,2048]{1,0:T(8,128)S(1)}, u32[]{:S(2)}, u32[]{:S(2)}) collective-permute-start(f32[128,2048]{1,0:T(8,128)S(1)} %constant_dynamic-update-slice_fusion.18.refs_0_), channel_id=1, source_target_pairs={{0,1},{1,0},{2,3},{3,2},{4,5},{5,4},{6,7},{7,6},{8,9},{9,8},{10,11... | collective-permute-start | bytes 3145736 | tf_op jit(solution)/shard_map/ppermute | solution.py:109
  69.5 31.4 %collective-permute-start.26 = (f32[128,2048]{1,0:T(8,128)S(1)}, f32[128,2048]{1,0:T(8,128)S(1)}, u32[]{:S(2)}, u32[]{:S(2)}) collective-permute-start(f32[128,2048]{1,0:T(8,128)S(1)} %constant_dynamic-update-slice_fusion.18.refs_0_), channel_id=1, source_target_pairs={{0,2},{1,3},{2,0},{3,1},{4,6},{5,7},{6,4},{7,5},{8,10},{9,11},{10,... | collective-permute-start | bytes 3145736 | tf_op jit(solution)/shard_map/ppermute | solution.py:109
  78.5 13.0 %collective-permute-start.19 = (f32[32,1536]{1,0:T(8,128)S(1)}, f32[32,1536]{1,0:T(8,128)S(1)}, u32[]{:S(2)}, u32[]{:S(2)}) collective-permute-start(f32[32,1536]{1,0:T(8,128)S(1)} %slice.132), channel_id=1, source_target_pairs={{0,4},{1,5},{2,6},{3,7},{4,8},{5,9},{6,10},{7,11},{8,12},{9,13},{1... | collective-permute-start | bytes 589832 | tf_op jit(solution)/shard_map/ppermute | solution.py:128
  78.5 11.7 %collective-permute-start.20 = (f32[32,1536]{1,0:T(8,128)S(1)}, f32[32,1536]{1,0:T(8,128)S(1)}, u32[]{:S(2)}, u32[]{:S(2)}) collective-permute-start(f32[32,1536]{1,0:T(8,128)S(1)} %slice.132), channel_id=1, source_target_pairs={{0,8},{1,9},{2,10},{3,11},{4,12},{5,13},{6,14},{7,15},{8,0},{9,1},... | collective-permute-start | bytes 589832 | tf_op jit(solution)/shard_map/ppermute | solution.py:128
  79.7 16.4 %collective-permute-start.21 = (f32[32,1536]{1,0:T(8,128)S(1)}, f32[32,1536]{1,0:T(8,128)S(1)}, u32[]{:S(2)}, u32[]{:S(2)}) collective-permute-start(f32[32,1536]{1,0:T(8,128)S(1)} %slice.132), channel_id=1, source_target_pairs={{0,12},{1,13},{2,14},{3,15},{4,0},{5,1},{6,2},{7,3},{8,4},{9,5},{1... | collective-permute-start | bytes 589832 | tf_op jit(solution)/shard_map/ppermute | solution.py:128
  90.3 23.9 %collective-permute-start.33 = (f32[128,1024]{1,0:T(8,128)S(1)}, f32[128,1024]{1,0:T(8,128)S(1)}, u32[]{:S(2)}, u32[]{:S(2)}) collective-permute-start(f32[128,1024]{1,0:T(8,128)S(1)} %slice_dynamic-update-slice_fusion.5.refs_0_), channel_id=1, source_target_pairs={{0,4},{1,5},{2,6},{3,7},{4,8},{5,9},{6,10},{7,11},{8,12},{9,13},{1... | collective-permute-start | bytes 1572872 | tf_op jit(solution)/shard_map/ppermute | solution.py:109
  91.5 48.3 %collective-permute-start.35 = (f32[128,1024]{1,0:T(8,128)S(1)}, f32[128,1024]{1,0:T(8,128)S(1)}, u32[]{:S(2)}, u32[]{:S(2)}) collective-permute-start(f32[128,1024]{1,0:T(8,128)S(1)} %slice_dynamic-update-slice_fusion.5.refs_0_), channel_id=1, source_target_pairs={{0,12},{1,13},{2,14},{3,15},{4,0},{5,1},{6,2},{7,3},{8,4},{9,5},{1... | collective-permute-start | bytes 1572872 | tf_op jit(solution)/shard_map/ppermute | solution.py:109
  101.0 13.4 %collective-permute-start.29 = (f32[64,2048]{1,0:T(8,128)S(1)}, f32[64,2048]{1,0:T(8,128)S(1)}, u32[]{:S(2)}, u32[]{:S(2)}) collective-permute-start(f32[64,2048]{1,0:T(8,128)S(1)} %slice.124), channel_id=1, source_target_pairs={{0,1},{1,0},{2,3},{3,2},{4,5},{5,4},{6,7},{7,6},{8,9},{9,8},{10,11... | collective-permute-start | bytes 1572872 | tf_op jit(solution)/shard_map/ppermute | solution.py:109
  102.2 12.2 %collective-permute-start.30 = (f32[64,2048]{1,0:T(8,128)S(1)}, f32[64,2048]{1,0:T(8,128)S(1)}, u32[]{:S(2)}, u32[]{:S(2)}) collective-permute-start(f32[64,2048]{1,0:T(8,128)S(1)} %slice.125), channel_id=1, source_target_pairs={{0,2},{1,3},{2,0},{3,1},{4,6},{5,7},{6,4},{7,5},{8,10},{9,11},{10,... | collective-permute-start | bytes 1572872 | tf_op jit(solution)/shard_map/ppermute | solution.py:109
  103.5 21.9 %collective-permute-start.27 = (f32[128,1536]{1,0:T(8,128)S(1)}, f32[128,1536]{1,0:T(8,128)S(1)}, u32[]{:S(2)}, u32[]{:S(2)}) collective-permute-start(f32[128,1536]{1,0:T(8,128)S(1)} %constant_dynamic-update-slice_fusion.14.refs_0_), channel_id=1, source_target_pairs={{0,1},{1,0},{2,3},{3,2},{4,5},{5,4},{6,7},{7,6},{8,9},{9,8},{10,11... | collective-permute-start | bytes 2359304 | tf_op jit(solution)/shard_map/ppermute | solution.py:109
  114.2 12.0 %collective-permute-start.28 = (f32[128,1536]{1,0:T(8,128)S(1)}, f32[128,1536]{1,0:T(8,128)S(1)}, u32[]{:S(2)}, u32[]{:S(2)}) collective-permute-start(f32[128,1536]{1,0:T(8,128)S(1)} %constant_dynamic-update-slice_fusion.14.refs_0_), channel_id=1, source_target_pairs={{0,2},{1,3},{2,0},{3,1},{4,6},{5,7},{6,4},{7,5},{8,10},{9,11},{10,... | collective-permute-start | bytes 2359304 | tf_op jit(solution)/shard_map/ppermute | solution.py:109
  114.4 25.5 %collective-permute-start.34 = (f32[128,1024]{1,0:T(8,128)S(1)}, f32[128,1024]{1,0:T(8,128)S(1)}, u32[]{:S(2)}, u32[]{:S(2)}) collective-permute-start(f32[128,1024]{1,0:T(8,128)S(1)} %collective-permute-done.33.refs_1_), channel_id=1, source_target_pairs={{0,4},{1,5},{2,6},{3,7},{4,8},{5,9},{6,10},{7,11},{8,12},{9,13},{1... | collective-permute-start | bytes 1572872 | tf_op jit(solution)/shard_map/ppermute | solution.py:109
  126.2 23.9 %collective-permute-start.31 = (f32[64,1536]{1,0:T(8,128)S(1)}, f32[64,1536]{1,0:T(8,128)S(1)}, u32[]{:S(2)}, u32[]{:S(2)}) collective-permute-start(f32[64,1536]{1,0:T(8,128)S(1)} %slice.126), channel_id=1, source_target_pairs={{0,1},{1,0},{2,3},{3,2},{4,5},{5,4},{6,7},{7,6},{8,9},{9,8},{10,11... | collective-permute-start | bytes 1179656 | tf_op jit(solution)/shard_map/ppermute | solution.py:109
  127.8 22.3 %collective-permute-start.32 = (f32[64,1536]{1,0:T(8,128)S(1)}, f32[64,1536]{1,0:T(8,128)S(1)}, u32[]{:S(2)}, u32[]{:S(2)}) collective-permute-start(f32[64,1536]{1,0:T(8,128)S(1)} %slice.127), channel_id=1, source_target_pairs={{0,2},{1,3},{2,0},{3,1},{4,6},{5,7},{6,4},{7,5},{8,10},{9,11},{10,... | collective-permute-start | bytes 1179656 | tf_op jit(solution)/shard_map/ppermute | solution.py:109
  150.1 27.4 %copy-start.3 = (f32[512,256]{1,0:T(8,128)S(1)}, f32[512,256]{1,0:T(8,128)}, u32[]{:S(2)}) copy-start(f32[512,256]{1,0:T(8,128)} %copy-done.2) | copy-start | bytes 1572868
  164.3 15.2 %copy-start.1 = (f32[256,896]{1,0:T(8,128)S(1)}, f32[256,896]{1,0:T(8,128)}, u32[]{:S(2)}) copy-start(f32[256,896]{1,0:T(8,128)} %param.7) | copy-start | bytes 2752516
  164.3 13.2 %collective-permute-start.36 = (f32[512,896]{1,0:T(8,128)S(1)}, f32[512,896]{1,0:T(8,128)S(1)}, u32[]{:S(2)}, u32[]{:S(2)}) collective-permute-start(f32[512,896]{1,0:T(8,128)S(1)} %get-tuple-element.65), channel_id=1, source_target_pairs={{0,16},{16,0},{1,17},{17,1},{2,18},{18,2},{3,19},{19,3},{4,20},{20... | collective-permute-start | bytes 5505032 | tf_op jit(solution)/shard_map/ppermute | solution.py:113
